TPU v7x, 256 devices: a whole 4x4x8 slice. The times are simulated.
256 devices in a mesh: dp: 4 (over y_lo, core), mp: 64 (over x, y_hi, z).
Axes of the slice: x: 4, y: 4 (y_hi: 2, y_lo: 2; y = y_hi * 2 + y_lo), z: 8, core: 2. Of those that a mesh axis runs over, the one named last changes fastest.
Arguments:
- queries: bfloat16 [12288, 256], P('mp'), may hold values from -6 to 6
- keys: bfloat16 [4, 4096, 4096], P('dp', 'mp'), may hold values from -6 to 6
- values: bfloat16 [4, 4096, 4096], P('dp', 'mp'), may hold values from -5.5 to 5.5
- out_cotangent: bfloat16 [4, 12288, 256], P('dp', 'mp'), may hold values from -356.20202 to 356.20202
Outputs:
- query_gradient: float32 [12288, 256], P('mp')
- key_gradient: bfloat16 [4, 4096, 4096], P('dp', 'mp')
- value_gradient: bfloat16 [4, 4096, 4096], P('dp', 'mp')
All inputs are finite; a program needn't handle non-finite values.
Results may differ from a plain program's by a relative error of at most 0.02.
Values may be sent and summed in bfloat16 or wider, within the bound.
A program may use at most 64 MiB of HBM per device.

v0:
```python
import math

import jax
import jax.numpy as jnp
from jax import lax
from jax.sharding import PartitionSpec as P

HEADS = 16


def unchanged(array):
    return array


def attend(query_heads, cotangent_heads, key_here, value_here, merge_top, merge_delta):
    heads_here, head_rows, head_size = query_heads.shape
    total_keys = key_here.shape[0]
    score_scale = 1.0 / math.sqrt(head_size)
    block_size = math.gcd(total_keys, 1024)
    block_count = total_keys // block_size
    key_tiles = key_here.reshape(block_count, block_size, heads_here, head_size)
    value_tiles = value_here.reshape(block_count, block_size, heads_here, head_size)

    def logits_of(key_tile):
        return (
            jnp.einsum("hrd,khd->hrk", query_heads, key_tile, preferred_element_type=jnp.float32)
            * score_scale
        )

    def stats_step(running, key_tile):
        row_top, row_total = running
        logits = logits_of(key_tile)
        new_top = jnp.maximum(row_top, jnp.max(logits, axis=2))
        row_total = row_total * jnp.exp(row_top - new_top) + jnp.sum(
            jnp.exp(logits - new_top[:, :, None]), axis=2
        )
        return ((new_top, row_total), None)

    initial = (
        jnp.full((heads_here, head_rows), -jnp.inf, jnp.float32),
        jnp.zeros((heads_here, head_rows), jnp.float32),
    )
    (row_top, row_total), unused = lax.scan(stats_step, initial, key_tiles)
    log_total = merge_top(row_top + jnp.log(row_total))[:, :, None]

    def delta_step(delta_sum, tile_pair):
        key_tile, value_tile = tile_pair
        softmax_weights = jnp.exp(logits_of(key_tile) - log_total).astype(jnp.bfloat16)
        weight_cotangent = jnp.einsum(
            "hrd,khd->hrk", cotangent_heads, value_tile, preferred_element_type=jnp.float32
        )
        return (
            delta_sum + jnp.sum(softmax_weights.astype(jnp.float32) * weight_cotangent, axis=2),
            None,
        )

    row_delta, unused = lax.scan(
        delta_step, jnp.zeros((heads_here, head_rows), jnp.float32), (key_tiles, value_tiles)
    )
    row_delta = merge_delta(row_delta)[:, :, None]

    def gradient_step(query_sum, tile_pair):
        key_tile, value_tile = tile_pair
        weights = jnp.exp(logits_of(key_tile) - log_total)
        softmax_weights = weights.astype(jnp.bfloat16)
        weight_cotangent = jnp.einsum(
            "hrd,khd->hrk", cotangent_heads, value_tile, preferred_element_type=jnp.float32
        )
        score_cotangent = (weights * (weight_cotangent - row_delta)).astype(jnp.bfloat16)
        value_part = jnp.einsum(
            "hrk,hrd->khd", softmax_weights, cotangent_heads, preferred_element_type=jnp.float32
        )
        key_part = (
            jnp.einsum(
                "hrk,hrd->khd", score_cotangent, query_heads, preferred_element_type=jnp.float32
            )
            * score_scale
        )
        query_sum = query_sum + jnp.einsum(
            "hrk,khd->hrd", score_cotangent, key_tile, preferred_element_type=jnp.float32
        )
        return (query_sum, (key_part, value_part))

    query_sum, (key_parts, value_parts) = lax.scan(
        gradient_step,
        jnp.zeros((heads_here, head_rows, head_size), jnp.float32),
        (key_tiles, value_tiles),
    )
    width_here = heads_here * head_size
    return (
        query_sum * score_scale,
        key_parts.reshape(total_keys, width_here),
        value_parts.reshape(total_keys, width_here),
    )


def on_device(queries, keys, values, out_cotangent):
    mp_count = lax.axis_size("mp")
    heads_here = max(1, HEADS // mp_count)
    groups = max(1, mp_count // HEADS)
    block_rows, head_size = queries.shape
    head_rows = block_rows // heads_here
    tok_rows = keys.shape[1]
    full_width = keys.shape[2]
    total_keys = tok_rows * mp_count
    width_here = heads_here * head_size
    key_local = keys[0]
    value_local = values[0]
    key_send = jnp.repeat(key_local.reshape(tok_rows, HEADS, head_size), groups, axis=1)
    value_send = jnp.repeat(value_local.reshape(tok_rows, HEADS, head_size), groups, axis=1)
    key_got, value_got = (
        lax.all_to_all(key_send, "mp", split_axis=1, concat_axis=0, tiled=True),
        lax.all_to_all(value_send, "mp", split_axis=1, concat_axis=0, tiled=True),
    )
    key_here = key_got.reshape(total_keys, width_here)
    value_here = value_got.reshape(total_keys, width_here)
    query_heads = queries.reshape(heads_here, head_rows, head_size)
    cotangent_heads = out_cotangent[0].reshape(heads_here, head_rows, head_size)
    query_sum, key_partial, value_partial = attend(
        query_heads, cotangent_heads, key_here, value_here, unchanged, unchanged
    )
    query_local = query_sum.reshape(block_rows, head_size)
    key_back, value_back = (
        lax.all_to_all(
            key_partial.reshape(mp_count, tok_rows, width_here),
            "mp",
            split_axis=0,
            concat_axis=2,
            tiled=True,
        ),
        lax.all_to_all(
            value_partial.reshape(mp_count, tok_rows, width_here),
            "mp",
            split_axis=0,
            concat_axis=2,
            tiled=True,
        ),
    )
    key_gradient = (
        key_back.reshape(tok_rows, mp_count // groups, groups, width_here)
        .sum(axis=2)
        .reshape(tok_rows, full_width)
    )
    value_gradient = (
        value_back.reshape(tok_rows, mp_count // groups, groups, width_here)
        .sum(axis=2)
        .reshape(tok_rows, full_width)
    )
    query_gradient = lax.psum(query_local.astype(jnp.bfloat16), "dp").astype(jnp.float32)
    return (
        query_gradient,
        key_gradient.astype(jnp.bfloat16)[None],
        value_gradient.astype(jnp.bfloat16)[None],
    )


def solution(mesh):
    placed = (P("mp", None), P("dp", "mp", None), P("dp", "mp", None), P("dp", "mp", None))
    return jax.shard_map(
        on_device,
        mesh=mesh,
        in_specs=placed,
        out_specs=(P("mp", None), P("dp", "mp", None), P("dp", "mp", None)),
        check_vma=False,
    )
```

profile of v0, /device:TPU:1, one launch (start us, length us, event | category | flops | bytes accessed | tf_op | source)
XLA Modules:
  0.0 376.3 jit_solution(15135151563303244722)
XLA Ops:
  8.5 1.6 broadcast_in_dim.29
  10.1 15.1 %all-to-all-start = ((bf16[64,64,256]{2,0,1:T(8,128)(2,1)}), bf16[64,64,256]{2,0,1:T(8,128)(2,1)S(1)}, u32[]{:S(2)}, u32[]{:S(2)}) async-start(bf16[64,64,256]{2,0,1:T(8,128)(2,1)} %bitcast.171), calls=%async_computation | async-start | bytes 4194304 | tf_op jit(solution)/shard_map/all_to_all | solution.py:112
  25.5 48.6 %all-to-all-done = bf16[64,64,256]{2,0,1:T(8,128)(2,1)S(1)} async-done(((bf16[64,64,256]{2,0,1:T(8,128)(2,1)}), bf16[64,64,256]{2,0,1:T(8,128)(2,1)S(1)}, u32[]{:S(2)}, u32[]{:S(2)}) %all-to-all-start) | async-done | bytes 2097184 | tf_op jit(solution)/shard_map/all_to_all | solution.py:112
  74.2 1.6 broadcast_in_dim.32
  75.7 9.5 %all-to-all-start.1 = ((bf16[64,64,256]{2,0,1:T(8,128)(2,1)}), bf16[64,64,256]{2,0,1:T(8,128)(2,1)}, u32[]{:S(2)}, u32[]{:S(2)}) async-start(bf16[64,64,256]{2,0,1:T(8,128)(2,1)} %bitcast.170), calls=%async_computation.1 | async-start | bytes 4194304 | tf_op jit(solution)/shard_map/all_to_all | solution.py:113
  85.3 3.1 while.39
  88.4 44.9 %all-to-all-done.1 = bf16[64,64,256]{2,0,1:T(8,128)(2,1)} async-done(((bf16[64,64,256]{2,0,1:T(8,128)(2,1)}), bf16[64,64,256]{2,0,1:T(8,128)(2,1)}, u32[]{:S(2)}, u32[]{:S(2)}) %all-to-all-start.1) | async-done | bytes 2097184 | tf_op jit(solution)/shard_map/all_to_all | solution.py:113
  133.3 7.4 %while.40 = (s32[]{:T(128)}, f32[1,192]{1,0:T(1,128)S(1)}, bf16[4,1024,1,256]{3,1,2,0:T(8,128)(2,1)S(1)}, bf16[1,192,256]{2,1,0:T(8,128)(2,1)S(1)}, f32[1,192,1]...) while((s32[]{:T(128)}, f32[1,192]{1,0:T(1,128)S(1)}, ...), condition=%wide.region_6.7_spmd.clone, body=%wide.region_4.6_spmd.clone.sunk | while | flops 202506432 | bytes 2822263 | solution.py:57
  133.6 1.5 fusion.80
  135.5 1.5 fusion.80
  137.3 1.5 fusion.80
  139.2 1.5 fusion.80
  140.7 19.0 %while.41 = (s32[]{:T(128)}, f32[1,192,256]{2,1,0:T(8,128)S(1)}, f32[4,1024,1,256]{3,1,2,0:T(8,128)}, f32[4,1024,1,256]{3,1,2,0:T(8,128)}, bf16[4,1024,1,256]{3,...) while((s32[]{:T(128)}, f32[1,192,256]{2,1,0:T(8,128)S(1)}, ...), condition=%wide.region_8.9_spmd.clone, body=%wide.region_7.8_spmd.clone.sunk | while | flops 504856576 | bytes 7997339 | solution.py:84
  141.0 1.4 fusion.93
  145.8 1.4 fusion.93
  148.8 1.4 fusion.95
  150.6 1.4 fusion.93
  159.7 103.1 %all_to_all.60 = f32[64,64,256]{2,1,0:T(8,128)} all-to-all(f32[64,64,256]{2,1,0:T(8,128)} %bitcast.172), channel_id=1, replica_groups=mesh['dp'=4,'mp'=64] {'mp'}, dimensions={0} | all-to-all | bytes 8388608 | tf_op jit(solution)/shard_map/all_to_all | solution.py:131
  262.8 9.9 %all-to-all-start.2 = ((f32[64,64,256]{2,1,0:T(8,128)}), f32[64,64,256]{2,1,0:T(8,128)}, u32[]{:S(2)}, u32[]{:S(2)}) async-start(f32[64,64,256]{2,1,0:T(8,128)} %bitcast.173), calls=%async_computation.2 | async-start | bytes 8388608 | tf_op jit(solution)/shard_map/all_to_all | solution.py:124
  273.4 48.0 %all-reduce.2.cloned.1.call-done = bf16[192,256]{1,0:T(8,128)(2,1)} async-done(((bf16[192,256]{1,0:T(8,128)(2,1)}), bf16[192,256]{1,0:T(8,128)(2,1)}) %all-reduce.2.cloned.1.call-update) | async-done | bytes 98320 | tf_op jit(solution)/shard_map/psum | solution.py:149
  321.4 1.6 convert_element_type.55
  323.0 2.6 bitcast_reduce_fusion
  327.0 38.4 %all-to-all-done.2 = f32[64,64,256]{2,1,0:T(8,128)} async-done(((f32[64,64,256]{2,1,0:T(8,128)}), f32[64,64,256]{2,1,0:T(8,128)}, u32[]{:S(2)}, u32[]{:S(2)}) %all-to-all-start.2) | async-done | bytes 4194336 | tf_op jit(solution)/shard_map/all_to_all | solution.py:124
  365.4 2.6 bitcast_reduce_fusion.1
  (68 shorter events, 22.7 us)
Async XLA Ops:
  8.3 16.9 %copy-start.2 = (bf16[1,64,4096]{2,1,0:T(8,128)(2,1)S(1)}, bf16[1,64,4096]{2,1,0:T(8,128)(2,1)}, u32[]{:S(2)}) copy-start(bf16[1,64,4096]{2,1,0:T(8,128)(2,1)} %param.12) | copy-start | bytes 1572868
  10.1 64.1 %all-to-all-start = ((bf16[64,64,256]{2,0,1:T(8,128)(2,1)}), bf16[64,64,256]{2,0,1:T(8,128)(2,1)S(1)}, u32[]{:S(2)}, u32[]{:S(2)}) async-start(bf16[64,64,256]{2,0,1:T(8,128)(2,1)} %bitcast.171), calls=%async_computation | async-start | bytes 4194304 | tf_op jit(solution)/shard_map/all_to_all | solution.py:112
  25.3 59.9 %copy-start = (bf16[192,256]{1,0:T(8,128)(2,1)S(1)}, bf16[192,256]{1,0:T(8,128)(2,1)}, u32[]{:S(2)}) copy-start(bf16[192,256]{1,0:T(8,128)(2,1)} %param.10) | copy-start | bytes 294916
  75.7 57.5 %all-to-all-start.1 = ((bf16[64,64,256]{2,0,1:T(8,128)(2,1)}), bf16[64,64,256]{2,0,1:T(8,128)(2,1)}, u32[]{:S(2)}, u32[]{:S(2)}) async-start(bf16[64,64,256]{2,0,1:T(8,128)(2,1)} %bitcast.170), calls=%async_computation.1 | async-start | bytes 4194304 | tf_op jit(solution)/shard_map/all_to_all | solution.py:113
  85.3 48.0 %copy-start.1 = (bf16[1,192,256]{2,1,0:T(8,128)(2,1)S(1)}, bf16[1,192,256]{2,1,0:T(8,128)(2,1)}, u32[]{:S(2)}) copy-start(bf16[1,192,256]{2,1,0:T(8,128)(2,1)} %param.13) | copy-start | bytes 294916
  262.8 102.6 %all-to-all-start.2 = ((f32[64,64,256]{2,1,0:T(8,128)}), f32[64,64,256]{2,1,0:T(8,128)}, u32[]{:S(2)}, u32[]{:S(2)}) async-start(f32[64,64,256]{2,1,0:T(8,128)} %bitcast.173), calls=%async_computation.2 | async-start | bytes 8388608 | tf_op jit(solution)/shard_map/all_to_all | solution.py:124
  272.7 48.7 %all-reduce.2.cloned.1.call-start = ((), (), s32[]{:S(2)}) async-start(), calls=%async_computation.4 | async-start | bytes 196608 | tf_op jit(solution)/shard_map/psum | solution.py:149
Sparse Core Ops, SparseCore 0:
  276.7 44.6 all-reduce.1
where the time goes:
time: 381 us; the launch traced here: 376 us
  waiting for transfers between devices  180 us (47%)
  blocking collectives  103 us (27%)
  starting transfers between devices  34.5 us (9%)
  matrix products  27.9 us (7%)
  between operations  14.2 us (4%)
  other arithmetic  8.82 us (2%)
  local copies, waits for them, and re-layouts  7.44 us (2%)
    all_to_all x1, blocking collectives, on_device(): lax.all_to_all(value_partial.reshape(mp_count, tok_rows, width_here), 'mp...  103 us
    all_to_all x1, waiting for transfers between devices, on_device(): lax.all_to_all(key_send, 'mp', split_axis=1, concat_axis=0, tiled=True)  48.6 us
    psum x1, waiting for transfers between devices, on_device(): lax.psum(query_local.astype(jnp.bfloat16), 'dp').astype(jnp.float32)  48 us
    all_to_all x1, waiting for transfers between devices, on_device(): lax.all_to_all(value_send, 'mp', split_axis=1, concat_axis=0, tiled=True)  44.9 us
    all_to_all x1, waiting for transfers between devices, on_device(): lax.all_to_all(key_partial.reshape(mp_count, tok_rows, width_here), 'mp',...  38.4 us
    all_to_all x1, starting transfers between devices, on_device(): lax.all_to_all(key_send, 'mp', split_axis=1, concat_axis=0, tiled=True)  15.1 us
    all_to_all x1, starting transfers between devices, on_device(): lax.all_to_all(key_partial.reshape(mp_count, tok_rows, width_here), 'mp',...  9.91 us
    all_to_all x1, starting transfers between devices, on_device(): lax.all_to_all(value_send, 'mp', split_axis=1, concat_axis=0, tiled=True)  9.46 us
  transfers between devices with their start and end apart: 4, of which 4 were waited for; matrix products, arithmetic and copies ran while one was open for 3% of the time, Pallas kernels for 0%

commit v1 on v0

v1 whole, which is shorter than its diff:
```python
import math

import jax
import jax.numpy as jnp
from jax import lax
from jax.experimental import pallas as pl
from jax.experimental.pallas import tpu as pltpu
from jax.sharding import PartitionSpec as P

HEADS = 16
DH = 256
R = 768
DOCS = 4
MP = 64
Z = 8
K = MP // Z
PAIR = HEADS // K
BLOCK = 192
HALF = BLOCK // 2
POS = 64
HERE = K * POS
CHUNK = 256
CHUNKS = R // CHUNK
SCALE = 1.0 / math.sqrt(DH)
MESH = pl.DeviceIdType.MESH
F32 = jnp.float32
BF16 = jnp.bfloat16


def dot(a, b, dims):
    return lax.dot_general(a, b, (dims, ((), ())), preferred_element_type=F32)


def kernel(
    q_in, k_in, v_in, g_in,
    dq_out, dk_out, dv_out,
    kbuf, vbuf, qbuf, gbuf, pbuf, wbuf, p16, s16, dkst, dvst,
    dq32, dq16, crecv, zsend, zrecv, yrecv, mstat, lstat, dstat,
    own_sem, ksend, krecv, vsend, vrecv, qsend, qrecv, gsend, grecv,
    lsend, lrecv, dsend, drecv, dksend, dkrecv, dvsend, dvrecv,
    csend, crsem, zssem, zrsem, yssem, yrsem,
):
    dp, mp = lax.axis_index("dp"), lax.axis_index("mp")
    k, z = lax.div(mp, Z), lax.rem(mp, Z)
    core = lax.rem(dp, 2)
    sibling = dp + 1 - 2 * core
    right = k * Z + lax.rem(z + 1, Z)
    left = k * Z + lax.rem(z + Z - 1, Z)

    def remote(src, dst, ssem, rsem, where):
        return pltpu.make_async_remote_copy(
            src_ref=src, dst_ref=dst, send_sem=ssem, recv_sem=rsem, device_id=where, device_id_type=MESH
        )

    def mates(d):
        j = lax.rem(k + d, K)
        return j, (dp, j * Z + z)

    def ringmates(d):
        j = lax.rem(z + d, Z)
        return j, (dp, k * Z + j)

    def each(n, fn, first=1):
        def body(d, carry):
            fn(d)
            return carry

        lax.fori_loop(first, n, body, 0)

    barrier = pltpu.get_barrier_semaphore()

    def greet(where):
        pl.semaphore_signal(barrier, inc=1, device_id=where, device_id_type=MESH)

    each(K, lambda d: greet(mates(d)[1]))
    each(Z, lambda d: greet(ringmates(d)[1]))
    each(DOCS, lambda d: greet((lax.rem(dp + d, DOCS), mp)))
    pl.semaphore_wait(barrier, K - 1 + Z - 1 + DOCS - 1)

    streams = ((q_in, qbuf, qsend, qrecv), (g_in.at[0], gbuf, gsend, grecv))

    def rows_of(j, start=0, size=BLOCK):
        return pl.ds(pl.multiple_of(j * BLOCK + start, 32), size)

    def hop(stream, h, side):
        src_in, buf, ssem, rsem = stream
        j = lax.rem(z + (Z - h if side == 0 else h), Z)
        part = rows_of(j) if h < 3 else rows_of(j, side * HALF, HALF)
        src = src_in if h == 0 else buf.at[part]
        i = side * 4 + h
        return remote(src, buf.at[part], ssem.at[i], rsem.at[i], (dp, right if side == 0 else left))

    def key_copy(a, d):
        j, where = mates(d)
        src = k_in.at[0, :, pl.ds(pl.multiple_of((j * PAIR + a) * DH, DH), DH)]
        return remote(src, kbuf.at[a, pl.ds(pl.multiple_of(k * POS, POS), POS)], ksend.at[a, j], krecv.at[a, k], where)

    def value_copy(a, d):
        j, where = mates(d)
        src = v_in.at[0, :, pl.ds(pl.multiple_of((j * PAIR + a) * DH, DH), DH)]
        return remote(src, vbuf.at[a, pl.ds(pl.multiple_of(k * POS, POS), POS)], vsend.at[a, j], vrecv.at[a, k], where)

    for stream in streams:
        for side in range(2):
            hop(stream, 0, side).start()
    for a in range(PAIR):
        each(K, lambda d: key_copy(a, d).start())
        each(K, lambda d: value_copy(a, d).start())

    own = [
        pltpu.make_async_copy(q_in, qbuf.at[rows_of(z)], own_sem.at[0]),
        pltpu.make_async_copy(g_in.at[0], gbuf.at[rows_of(z)], own_sem.at[1]),
    ]
    for a in range(PAIR):
        cols = pl.ds(pl.multiple_of((k * PAIR + a) * DH, DH), DH)
        here = pl.ds(pl.multiple_of(k * POS, POS), POS)
        own.append(pltpu.make_async_copy(k_in.at[0, :, cols], kbuf.at[a, here], own_sem.at[2 + 2 * a]))
        own.append(pltpu.make_async_copy(v_in.at[0, :, cols], vbuf.at[a, here], own_sem.at[3 + 2 * a]))
    for copy in own:
        copy.start()

    for h in range(1, 4):
        for stream in streams:
            for side in range(2):
                hop(stream, h - 1, side).wait_recv()
                hop(stream, h, side).start()
    for copy in own:
        copy.wait()
    for stream in streams:
        for side in range(2):
            hop(stream, 3, side).wait_recv()
    for a in range(PAIR):
        def landed(d, a=a):
            j, where = mates(d)
            here = pl.ds(pl.multiple_of(j * POS, POS), POS)
            remote(kbuf.at[a, here], kbuf.at[a, here], ksend.at[a, j], krecv.at[a, j], where).wait_recv()
            remote(vbuf.at[a, here], vbuf.at[a, here], vsend.at[a, j], vrecv.at[a, j], where).wait_recv()

        each(K, landed)

    for a in range(PAIR):
        for c in range(CHUNKS):
            i = a * CHUNKS + c
            rows, cols = pl.ds(i * CHUNK, CHUNK), pl.ds(c * CHUNK, CHUNK)
            s = dot(kbuf[a], qbuf[rows, :], ((1,), (1,))) * SCALE
            top = jnp.max(s, axis=0, keepdims=True)
            p = jnp.exp(s - top)
            total = jnp.sum(p, axis=0, keepdims=True)
            w = dot(vbuf[a], gbuf[rows, :], ((1,), (1,)))
            delta = jnp.sum(p * w, axis=0, keepdims=True)
            pbuf[i] = p
            wbuf[i] = w
            mstat[a, :, cols] = top
            lstat[a, z, :, cols] = top + jnp.log(total)
            dstat[a, z, :, cols] = delta / total

        def stat_send(d, a=a):
            j, where = ringmates(d)
            remote(lstat.at[a, z], lstat.at[a, z], lsend.at[a, j], lrecv.at[a, z], where).start()
            remote(dstat.at[a, z], dstat.at[a, z], dsend.at[a, j], drecv.at[a, z], where).start()

        each(Z, stat_send)

    for a in range(PAIR):

        def stat_wait(d, a=a):
            j, where = ringmates(d)
            remote(lstat.at[a, j], lstat.at[a, j], lsend.at[a, j], lrecv.at[a, j], where).wait_recv()
            remote(dstat.at[a, j], dstat.at[a, j], dsend.at[a, j], drecv.at[a, j], where).wait_recv()

        each(Z, stat_wait)
        parts = [lstat[a, j] for j in range(Z)]
        peak = parts[0]
        for part in parts[1:]:
            peak = jnp.maximum(peak, part)
        shares = [jnp.exp(part - peak) for part in parts]
        whole = shares[0]
        for share in shares[1:]:
            whole = whole + share
        delta = shares[0] * dstat[a, 0]
        for j in range(1, Z):
            delta = delta + shares[j] * dstat[a, j]
        delta = delta / whole
        factor = jnp.exp(mstat[a] - (peak + jnp.log(whole)))
        for c in range(CHUNKS):
            i = a * CHUNKS + c
            rows = pl.ds(i * CHUNK, CHUNK)
            lo, hi = c * CHUNK, (c + 1) * CHUNK
            p = pbuf[i] * factor[:, lo:hi]
            s = (p * (wbuf[i] - delta[:, lo:hi])).astype(BF16)
            p16[a, :, lo:hi] = p.astype(BF16)
            s16[a, :, lo:hi] = s
            part = dot(s, kbuf[a], ((0,), (0,))) * SCALE
            dq32[rows, :] = part
            dq16[rows, :] = part.astype(BF16)

    def half_of(j, which):
        return pl.ds(pl.multiple_of(j * BLOCK + which * HALF, 32), HALF)

    def core_copy(j):
        return remote(dq16.at[half_of(j, 1 - core)], crecv.at[j], csend.at[j], crsem.at[j], (sibling, mp))

    each(Z, lambda j: core_copy(j).start(), 0)

    def key_back(a, d):
        j, where = mates(d)
        dst = dk_out.at[0, :, pl.ds(pl.multiple_of((k * PAIR + a) * DH, DH), DH)]
        src = dkst.at[a, pl.ds(pl.multiple_of(j * POS, POS), POS)]
        return remote(src, dst, dksend.at[a, j], dkrecv.at[a, k], where)

    def value_back(a, d):
        j, where = mates(d)
        dst = dv_out.at[0, :, pl.ds(pl.multiple_of((k * PAIR + a) * DH, DH), DH)]
        src = dvst.at[a, pl.ds(pl.multiple_of(j * POS, POS), POS)]
        return remote(src, dst, dvsend.at[a, j], dvrecv.at[a, k], where)

    kept = []
    for a in range(PAIR):
        rows = pl.ds(a * R, R)
        cols = pl.ds(pl.multiple_of((k * PAIR + a) * DH, DH), DH)
        here = pl.ds(pl.multiple_of(k * POS, POS), POS)
        dvst[a] = dot(p16[a], gbuf[rows, :], ((1,), (0,))).astype(BF16)
        each(K, lambda d, a=a: value_back(a, d).start())
        dkst[a] = (dot(s16[a], qbuf[rows, :], ((1,), (0,))) * SCALE).astype(BF16)
        each(K, lambda d, a=a: key_back(a, d).start())
        kept.append(pltpu.make_async_copy(dvst.at[a, here], dv_out.at[0, :, cols], own_sem.at[2 * a]))
        kept.append(pltpu.make_async_copy(dkst.at[a, here], dk_out.at[0, :, cols], own_sem.at[2 * a + 1]))
        for copy in kept[2 * a :]:
            copy.start()

    def z_copy(j):
        return remote(zsend.at[j], zrecv.at[z], zssem.at[j], zrsem.at[z], (dp, k * Z + j))

    def pass_on(d):
        j = lax.rem(z + d, Z)
        core_copy(j).wait_recv()
        zsend[j] = (dq32[half_of(j, core), :] + crecv[j].astype(F32)).astype(BF16)

        @pl.when(d < Z)
        def _():
            z_copy(j).start()

    each(Z + 1, pass_on)
    zrecv[z] = zsend[z]

    def z_wait(d):
        j = lax.rem(z + d, Z)
        remote(zsend.at[j], zrecv.at[j], zssem.at[j], zrsem.at[j], (dp, k * Z + j)).wait_recv()

    each(Z, z_wait)
    half_sum = zrecv[0].astype(F32)
    for j in range(1, Z):
        half_sum = half_sum + zrecv[j].astype(F32)
    yrecv[dp] = half_sum.astype(BF16)

    def y_copy(d):
        j = lax.rem(dp + d, DOCS)
        return remote(yrecv.at[dp], yrecv.at[dp], yssem.at[j], yrsem.at[dp], (j, mp))

    each(DOCS, lambda d: y_copy(d).start())

    def y_wait(d):
        j = lax.rem(dp + d, DOCS)
        remote(yrecv.at[j], yrecv.at[j], yssem.at[j], yrsem.at[j], (j, mp)).wait_recv()

    each(DOCS, y_wait)
    for h in range(2):
        dq_out[pl.ds(h * HALF, HALF), :] = yrecv[h].astype(F32) + yrecv[2 + h].astype(F32)

    for copy in kept:
        copy.wait()
    for stream in streams:
        for h in range(4):
            for side in range(2):
                hop(stream, h, side).wait_send()
    for a in range(PAIR):

        def settle(d, a=a):
            j, where = mates(d)
            cols = pl.ds(pl.multiple_of((j * PAIR + a) * DH, DH), DH)
            here = pl.ds(pl.multiple_of(j * POS, POS), POS)
            key_copy(a, d).wait_send()
            value_copy(a, d).wait_send()
            key_back(a, d).wait_send()
            value_back(a, d).wait_send()
            remote(dkst.at[a, here], dk_out.at[0, :, cols], dksend.at[a, j], dkrecv.at[a, j], where).wait_recv()
            remote(dvst.at[a, here], dv_out.at[0, :, cols], dvsend.at[a, j], dvrecv.at[a, j], where).wait_recv()

        each(K, settle)

        def settle_stats(d, a=a):
            j, where = ringmates(d)
            remote(lstat.at[a, z], lstat.at[a, z], lsend.at[a, j], lrecv.at[a, z], where).wait_send()
            remote(dstat.at[a, z], dstat.at[a, z], dsend.at[a, j], drecv.at[a, z], where).wait_send()

        each(Z, settle_stats)
    each(Z, lambda j: core_copy(j).wait_send(), 0)
    each(Z, lambda d: z_copy(lax.rem(z + d, Z)).wait_send())
    each(DOCS, lambda d: y_copy(d).wait_send())


def on_device(queries, keys, values, out_cotangent):
    anywhere = pl.BlockSpec(memory_space=pl.ANY)
    dma = pltpu.SemaphoreType.DMA
    return pl.pallas_call(
        kernel,
        out_shape=(
            jax.ShapeDtypeStruct((BLOCK, DH), F32),
            jax.ShapeDtypeStruct(keys.shape, BF16),
            jax.ShapeDtypeStruct(values.shape, BF16),
        ),
        in_specs=[anywhere] * 4,
        out_specs=(pl.BlockSpec(memory_space=pltpu.VMEM), anywhere, anywhere),
        scratch_shapes=[
            pltpu.VMEM((PAIR, HERE, DH), BF16),
            pltpu.VMEM((PAIR, HERE, DH), BF16),
            pltpu.VMEM((PAIR * R, DH), BF16),
            pltpu.VMEM((PAIR * R, DH), BF16),
            pltpu.VMEM((PAIR * CHUNKS, HERE, CHUNK), F32),
            pltpu.VMEM((PAIR * CHUNKS, HERE, CHUNK), F32),
            pltpu.VMEM((PAIR, HERE, R), BF16),
            pltpu.VMEM((PAIR, HERE, R), BF16),
            pltpu.VMEM((PAIR, HERE, DH), BF16),
            pltpu.VMEM((PAIR, HERE, DH), BF16),
            pltpu.VMEM((PAIR * R, DH), F32),
            pltpu.VMEM((PAIR * R, DH), BF16),
            pltpu.VMEM((Z, HALF, DH), BF16),
            pltpu.VMEM((Z, HALF, DH), BF16),
            pltpu.VMEM((Z, HALF, DH), BF16),
            pltpu.VMEM((DOCS, HALF, DH), BF16),
            pltpu.VMEM((PAIR, 1, R), F32),
            pltpu.VMEM((PAIR, Z, 1, R), F32),
            pltpu.VMEM((PAIR, Z, 1, R), F32),
            dma((6,)),
            dma((PAIR, K)), dma((PAIR, K)), dma((PAIR, K)), dma((PAIR, K)),
            dma((8,)), dma((8,)), dma((8,)), dma((8,)),
            dma((PAIR, Z)), dma((PAIR, Z)), dma((PAIR, Z)), dma((PAIR, Z)),
            dma((PAIR, K)), dma((PAIR, K)), dma((PAIR, K)), dma((PAIR, K)),
            dma((Z,)), dma((Z,)), dma((Z,)), dma((Z,)), dma((DOCS,)), dma((DOCS,)),
        ],
        compiler_params=pltpu.CompilerParams(
            collective_id=0, has_side_effects=True, vmem_limit_bytes=48 * 2**20
        ),
        cost_estimate=pl.CostEstimate(
            flops=10 * HERE * PAIR * R * DH, bytes_accessed=4 * 2**20, transcendentals=HERE * PAIR * R
        ),
    )(queries, keys, values, out_cotangent)


def solution(mesh):
    placed = (P("mp", None), P("dp", "mp", None), P("dp", "mp", None), P("dp", "mp", None))
    return jax.shard_map(
        on_device,
        mesh=mesh,
        in_specs=placed,
        out_specs=(P("mp", None), P("dp", "mp", None), P("dp", "mp", None)),
        check_vma=False,
    )
```

time: 381 us -> 63.7 us (0.17); the launches traced: 376 us -> 63.5 us
  waiting for transfers between devices: 180 us -> 0 us
  blocking collectives: 103 us -> 0 us
  Pallas kernels: 0 us -> 56.7 us
  starting transfers between devices: 34.5 us -> 0 us
  matrix products: 27.9 us -> 0 us
  between operations: 14.2 us -> 0.65 us
  other arithmetic: 8.82 us -> 0 us
    all_to_all x3 -> x0, waiting for transfers between devices: 132 us -> none  [the longest x1 48.6 us: on_device(): lax.all_to_all(key_send, 'mp', split_axis=1, concat_axis=0, tiled=True)]
    all_to_all x1 -> x0, blocking collectives: 103 us -> none  [on_device(): lax.all_to_all(value_partial.reshape(mp_count, tok_rows, width_here), 'mp...]
    pallas_call x0 -> x1, Pallas kernels: none -> 56.7 us  [on_device(): pl.pallas_call(kernel, out_shape=(jax.ShapeDtypeStruct((BLOCK, DH), F32),...]
    psum x1 -> x0, waiting for transfers between devices: 48 us -> none  [on_device(): lax.psum(query_local.astype(jnp.bfloat16), 'dp').astype(jnp.float32)]
    all_to_all x3 -> x0, starting transfers between devices: 34.5 us -> none  [the longest x1 15.1 us: on_device(): lax.all_to_all(key_send, 'mp', split_axis=1, concat_axis=0, tiled=True)]
    dot_general x32 -> x0, matrix products: 27.9 us -> none  [the longest x4 5.88 us: delta_step(): jnp.einsum('hrd,khd->hrk', cotangent_heads, value_tile, preferred_element...]
    reduce_sum x6 -> x0, other arithmetic: 6.42 us -> none  [the longest x1 2.65 us: on_device(): key_gradient = key_back.reshape(tok_rows, mp_count // groups, groups, wid...]
    unnamed x8 -> x11, local copies, waits for them, and re-layouts: 1.27 us -> 6.12 us
  transfers between devices with their start and end apart: 4 -> 0, of which waited for: 4 -> 0; matrix products, arithmetic and copies ran while one was open for 3% -> 0% of each run, Pallas kernels for 0% -> 0%
where the time goes in v1:
time: 63.7 us; the launch traced here: 63.5 us
  Pallas kernels  56.7 us (89%)
  local copies, waits for them, and re-layouts  6.12 us (10%)
  between operations  0.65 us (1%)
    pallas_call x1, Pallas kernels, on_device(): pl.pallas_call(kernel, out_shape=(jax.ShapeDtypeStruct((BLOCK, DH), F32),...  56.7 us
    unnamed x11, local copies, waits for them, and re-layouts  6.12 us

profile of v1, /device:TPU:1, one launch (start us, length us, event | category | flops | bytes accessed | tf_op | source)
XLA Modules:
  0.0 63.5 jit_solution(1659207080855858914)
XLA Ops:
  0.6 0.0 copy-start
  0.6 1.0 %copy-done = bf16[1,64,4096]{2,1,0:T(8,128)(2,1)S(1)} copy-done((bf16[1,64,4096]{2,1,0:T(8,128)(2,1)S(1)}, bf16[1,64,4096]{2,1,0:T(8,128)(2,1)}, u32[]{:S(2)}) %copy-start) | copy-done | bytes 524312
  1.7 0.0 copy-start.1
  1.7 1.0 %copy-done.1 = bf16[1,64,4096]{2,1,0:T(8,128)(2,1)S(1)} copy-done((bf16[1,64,4096]{2,1,0:T(8,128)(2,1)S(1)}, bf16[1,64,4096]{2,1,0:T(8,128)(2,1)}, u32[]{:S(2)}) %copy-start.1) | copy-done | bytes 524312
  2.7 0.0 copy-start.2
  2.7 0.9 %copy-done.2 = bf16[192,256]{1,0:T(8,128)(2,1)S(1)} copy-done((bf16[192,256]{1,0:T(8,128)(2,1)S(1)}, bf16[192,256]{1,0:T(8,128)(2,1)}, u32[]{:S(2)}) %copy-start.2) | copy-done | bytes 98328
  3.6 0.0 copy-start.3
  3.6 0.9 %copy-done.3 = bf16[1,192,256]{2,1,0:T(8,128)(2,1)S(1)} copy-done((bf16[1,192,256]{2,1,0:T(8,128)(2,1)S(1)}, bf16[1,192,256]{2,1,0:T(8,128)(2,1)}, u32[]{:S(2)}) %copy-start.3) | copy-done | bytes 98328
  4.5 56.7 %shard_map.67 = (f32[192,256]{1,0:T(8,128)S(1)}, bf16[1,64,4096]{2,1,0:T(8,128)(2,1)S(1)}, bf16[1,64,4096]{2,1,0:T(8,128)(2,1)S(1)}) custom-call(bf16[192,256]{1,0:T(8,128)(2,1)S(1)} %copy-done.2, bf16[1,64,4096]{2,1,0:T(8,128)(2,1)S(1)} %copy-done, bf16[1,64,4096]{2,1,0:T(8,128)(2,1)S(1)} %copy-done.1, bf16[1,192,256]{2,1,0:T(8,128)(2,1)S(1)} %copy-done.3), custom_call_target="tpu_custom_call" | custom-call | flops 2013265920 | bytes 4194304 | tf_op jit(solution)/shard_map/pallas_call | solution.py:305
  61.2 0.7 %copy.10 = f32[192,256]{1,0:T(8,128)} copy(f32[192,256]{1,0:T(8,128)S(1)} %get-tuple-element.6) | data formatting | bytes 393216
  61.9 0.8 %copy.11 = bf16[1,64,4096]{2,1,0:T(8,128)(2,1)} copy(bf16[1,64,4096]{2,1,0:T(8,128)(2,1)S(1)} %get-tuple-element.7) | data formatting | bytes 1048576
  62.7 0.8 %copy.12 = bf16[1,64,4096]{2,1,0:T(8,128)(2,1)} copy(bf16[1,64,4096]{2,1,0:T(8,128)(2,1)S(1)} %get-tuple-element.8) | data formatting | bytes 1048576
Async XLA Ops:
  0.6 1.0 %copy-start = (bf16[1,64,4096]{2,1,0:T(8,128)(2,1)S(1)}, bf16[1,64,4096]{2,1,0:T(8,128)(2,1)}, u32[]{:S(2)}) copy-start(bf16[1,64,4096]{2,1,0:T(8,128)(2,1)} %k_in.1) | copy-start | bytes 1572868
  1.7 1.0 %copy-start.1 = (bf16[1,64,4096]{2,1,0:T(8,128)(2,1)S(1)}, bf16[1,64,4096]{2,1,0:T(8,128)(2,1)}, u32[]{:S(2)}) copy-start(bf16[1,64,4096]{2,1,0:T(8,128)(2,1)} %v_in.1) | copy-start | bytes 1572868
  2.7 0.9 %copy-start.2 = (bf16[192,256]{1,0:T(8,128)(2,1)S(1)}, bf16[192,256]{1,0:T(8,128)(2,1)}, u32[]{:S(2)}) copy-start(bf16[192,256]{1,0:T(8,128)(2,1)} %q_in.1) | copy-start | bytes 294916
  3.6 0.9 %copy-start.3 = (bf16[1,192,256]{2,1,0:T(8,128)(2,1)S(1)}, bf16[1,192,256]{2,1,0:T(8,128)(2,1)}, u32[]{:S(2)}) copy-start(bf16[1,192,256]{2,1,0:T(8,128)(2,1)} %g_in.1) | copy-start | bytes 294916

commit v2 on v1

v2 whole, which is shorter than its diff:
```python
import math

import jax
import jax.numpy as jnp
from jax import lax
from jax.experimental import pallas as pl
from jax.experimental.pallas import tpu as pltpu
from jax.sharding import PartitionSpec as P

HEADS = 16
DH = 256
R = 768
DOCS = 4
MP = 64
Z = 8
K = MP // Z
PAIR = HEADS // K
BLOCK = 192
HALF = BLOCK // 2
POS = 64
HERE = K * POS
CHUNK = 256
CHUNKS = R // CHUNK
SCALE = 1.0 / math.sqrt(DH)
MESH = pl.DeviceIdType.MESH
F32 = jnp.float32
BF16 = jnp.bfloat16


def dot(a, b, dims):
    return lax.dot_general(a, b, (dims, ((), ())), preferred_element_type=F32)


def kernel(
    q_in, k_in, v_in, g_in,
    yrecv, dk_out, dv_out,
    kbuf, vbuf, qbuf, gbuf, pbuf, wbuf, p16, s16, dkst, dvst,
    dq32, dq16, crecv, zsend, zrecv, mstat, stat,
    own_sem, ksem, vsem, rsend, rrecv, shsem, stsem, dksem, dvsem, csend, crsem, zsem, ysem,
):
    dp, mp = lax.axis_index("dp"), lax.axis_index("mp")
    k, z = lax.div(mp, Z), lax.rem(mp, Z)
    core = lax.rem(dp, 2)
    sibling = dp + 1 - 2 * core
    right = k * Z + lax.rem(z + 1, Z)
    left = k * Z + lax.rem(z + Z - 1, Z)

    def remote(src, dst, ssem, rsem, where):
        return pltpu.make_async_remote_copy(
            src_ref=src, dst_ref=dst, send_sem=ssem, recv_sem=rsem, device_id=where, device_id_type=MESH
        )

    def mate(d):
        j = lax.rem(k + d, K)
        return j, (dp, j * Z + z)

    def ringmate(d):
        j = lax.rem(z + d, Z)
        return j, (dp, k * Z + j)

    def doc(d):
        j = lax.rem(dp + d, DOCS)
        return j, (j, mp)

    barrier = pltpu.get_barrier_semaphore()
    for others, count in ((mate, K), (ringmate, Z), (doc, DOCS)):
        for d in range(1, count):
            pl.semaphore_signal(barrier, inc=1, device_id=others(d)[1], device_id_type=MESH)
    pl.semaphore_wait(barrier, K - 1 + Z - 1 + DOCS - 1)

    def rows_of(j, start, size):
        return pl.ds(pl.multiple_of(j * BLOCK + start, 16), size)

    def cols_of(j):
        return pl.ds(pl.multiple_of(j * PAIR * DH, PAIR * DH), PAIR * DH)

    def pos_of(j):
        return pl.ds(pl.multiple_of(j * POS, POS), POS)

    def hop(part, h, side):
        buf, first = (qbuf, q_in) if part == 0 else (gbuf, g_in.at[0])
        start, size = (core * HALF, HALF) if part == 0 else ((part - 1) * HALF, HALF)
        if h == 3 and part == 0:
            start, size = start + side * (HALF // 2), HALF // 2
        j = lax.rem(z + (Z - h if side == 0 else h), Z)
        there = buf.at[rows_of(j, start, size)]
        src = first.at[pl.ds(pl.multiple_of(start, 16), size)] if h == 0 else there
        i = (part * 2 + side) * 4 + h
        return remote(src, there, rsend.at[i], rrecv.at[i], (dp, right if side == 0 else left))

    def travels(part, h, side):
        return h < 3 or part == 0 or part == side + 1

    def share(h, side):
        j = lax.rem(z + (Z - 1 - h if side == 0 else h + 1), Z)
        start, size = (core * HALF, HALF) if h < 3 else (core * HALF + side * (HALF // 2), HALF // 2)
        there = qbuf.at[rows_of(j, start, size)]
        return remote(there, there, shsem.at[0], shsem.at[1], (sibling, mp))

    def shared():
        there = qbuf.at[pl.ds(0, (Z - 1) * HALF)]
        return remote(there, there, shsem.at[0], shsem.at[1], (sibling, mp))

    for part in range(3):
        for side in range(2):
            hop(part, 0, side).start()

    for src, buf, sem in ((k_in, kbuf, ksem), (v_in, vbuf, vsem)):
        for d in range(1, K):
            j, where = mate(d)
            remote(src.at[0, :, cols_of(j)], buf.at[pos_of(k)], sem.at[0], sem.at[1], where).start()

    own = [
        pltpu.make_async_copy(q_in, qbuf.at[rows_of(z, 0, BLOCK)], own_sem.at[0]),
        pltpu.make_async_copy(g_in.at[0], gbuf.at[rows_of(z, 0, BLOCK)], own_sem.at[1]),
        pltpu.make_async_copy(k_in.at[0, :, cols_of(k)], kbuf.at[pos_of(k)], own_sem.at[2]),
        pltpu.make_async_copy(v_in.at[0, :, cols_of(k)], vbuf.at[pos_of(k)], own_sem.at[3]),
    ]
    for copy in own:
        copy.start()

    for h in range(1, 5):
        for part in range(3):
            for side in range(2):
                if travels(part, h - 1, side):
                    hop(part, h - 1, side).wait_recv()
                    if h < 4 and travels(part, h, side):
                        hop(part, h, side).start()
                    if part == 0:
                        share(h - 1, side).start()

    def all_mates(buf, sem):
        there = buf.at[pl.ds(0, (K - 1) * POS)]
        return remote(there, there, sem.at[0], sem.at[1], mate(1)[1])

    for copy in own:
        copy.wait()
    shared().wait_recv()
    all_mates(kbuf, ksem).wait_recv()
    all_mates(vbuf, vsem).wait_recv()

    for a in range(PAIR):
        head = pl.ds(a * DH, DH)
        for c in range(CHUNKS):
            i = a * CHUNKS + c
            rows, cols = pl.ds(i * CHUNK, CHUNK), pl.ds(c * CHUNK, CHUNK)
            s = dot(kbuf[:, head], qbuf[rows, :], ((1,), (1,))) * SCALE
            top = jnp.max(s, axis=0, keepdims=True)
            p = jnp.exp(s - top)
            total = jnp.sum(p, axis=0, keepdims=True)
            w = dot(vbuf[:, head], gbuf[rows, :], ((1,), (1,)))
            delta = jnp.sum(p * w, axis=0, keepdims=True)
            pbuf[i] = p
            wbuf[i] = w
            mstat[a, :, cols] = top
            stat[z, 2 * a, :, cols] = top + jnp.log(total)
            stat[z, 2 * a + 1, :, cols] = delta / total

    for d in (4, 3, 5, 2, 6, 1, 7):
        j, where = ringmate(d)
        remote(stat.at[z], stat.at[z], stsem.at[0], stsem.at[1], where).start()

    def all_stats():
        there = stat.at[pl.ds(0, Z - 1)]
        return remote(there, there, stsem.at[0], stsem.at[1], ringmate(1)[1])

    all_stats().wait_recv()

    def core_copy(a):
        mine = pl.ds(pl.multiple_of((1 - core) * HALF, HALF), HALF)
        there = pl.ds(a * (Z // 2), Z // 2)
        return remote(dq16.at[there, mine], crecv.at[there], csend.at[a], crsem.at[a], (sibling, mp))

    for a in range(PAIR):
        head = pl.ds(a * DH, DH)
        parts = [stat[j, 2 * a] for j in range(Z)]
        peak = parts[0]
        for part in parts[1:]:
            peak = jnp.maximum(peak, part)
        shares = [jnp.exp(part - peak) for part in parts]
        whole = shares[0]
        for part in shares[1:]:
            whole = whole + part
        delta = shares[0] * stat[0, 2 * a + 1]
        for j in range(1, Z):
            delta = delta + shares[j] * stat[j, 2 * a + 1]
        delta = delta / whole
        factor = jnp.exp(mstat[a] - (peak + jnp.log(whole)))
        for c in range(CHUNKS):
            i = a * CHUNKS + c
            lo, hi = c * CHUNK, (c + 1) * CHUNK
            p = pbuf[i] * factor[:, lo:hi]
            p16[a, :, lo:hi] = p.astype(BF16)
            s16[a, :, lo:hi] = (p * (wbuf[i] - delta[:, lo:hi])).astype(BF16)
        there = pl.ds(a * (Z // 2), Z // 2)
        part = (dot(s16[a], kbuf[:, head], ((0,), (0,))) * SCALE).reshape(Z // 2, BLOCK, DH)
        dq32[there] = part
        dq16[there] = part.astype(BF16)
        core_copy(a).start()

    def back(stage, out, sem, values_of):
        for a in range(PAIR):
            stage[:, a * DH : (a + 1) * DH] = values_of(a).astype(BF16)
        for d in range(1, K):
            j, where = mate(d)
            remote(stage.at[pos_of(j)], out.at[0, :, cols_of(k)], sem.at[0], sem.at[1], where).start()

    back(dvst, dv_out, dvsem, lambda a: dot(p16[a], gbuf[pl.ds(a * R, R), :], ((1,), (0,))))

    def z_copy(j):
        return remote(zsend.at[j], zrecv.at[z], zsem.at[0], zsem.at[1], (dp, k * Z + j))

    for a in range(PAIR):
        core_copy(a).wait_recv()
    for d in (4, 3, 5, 2, 6, 1, 7, 0):
        j = lax.rem(z + d, Z)
        mine = pl.ds(pl.multiple_of(core * HALF, HALF), HALF)
        part = (dq32[j, mine, :] + crecv[j].astype(F32)).astype(BF16)
        if d:
            zsend[j] = part
            z_copy(j).start()
        else:
            zrecv[j] = part

    back(dkst, dk_out, dksem, lambda a: dot(s16[a], qbuf[pl.ds(a * R, R), :], ((1,), (0,))) * SCALE)
    kept = [
        pltpu.make_async_copy(dvst.at[pos_of(k)], dv_out.at[0, :, cols_of(k)], own_sem.at[0]),
        pltpu.make_async_copy(dkst.at[pos_of(k)], dk_out.at[0, :, cols_of(k)], own_sem.at[1]),
    ]
    for copy in kept:
        copy.start()

    for part in range(3):
        for h in range(4):
            for side in range(2):
                if travels(part, h, side):
                    hop(part, h, side).wait_send()
    shared().wait_send()
    all_mates(kbuf, ksem).wait_send()
    all_mates(vbuf, vsem).wait_send()
    all_stats().wait_send()
    for a in range(PAIR):
        core_copy(a).wait_send()

    def all_z():
        there = zrecv.at[pl.ds(0, Z - 1)]
        return remote(there, there, zsem.at[0], zsem.at[1], ringmate(1)[1])

    all_z().wait_recv()
    half_sum = zrecv[0].astype(F32)
    for j in range(1, Z):
        half_sum = half_sum + zrecv[j].astype(F32)
    yrecv[dp] = half_sum.astype(BF16)

    for d in range(1, DOCS):
        remote(yrecv.at[dp], yrecv.at[dp], ysem.at[0], ysem.at[1], doc(d)[1]).start()

    def all_docs():
        there = yrecv.at[pl.ds(0, DOCS - 1)]
        return remote(there, there, ysem.at[0], ysem.at[1], doc(1)[1])

    all_docs().wait_recv()
    for copy in kept:
        copy.wait()
    for out, sem in ((dv_out, dvsem), (dk_out, dksem)):
        there = out.at[0, :, pl.ds(0, (K - 1) * PAIR * DH)]
        done = remote(there, there, sem.at[0], sem.at[1], mate(1)[1])
        done.wait_send()
        done.wait_recv()
    all_z().wait_send()
    all_docs().wait_send()


def finish(parts, dk_in, dv_in, dq_out, dk_out, dv_out, sem):
    copies = [
        pltpu.make_async_copy(dk_in, dk_out, sem.at[0]),
        pltpu.make_async_copy(dv_in, dv_out, sem.at[1]),
    ]
    for copy in copies:
        copy.start()
    for h in range(2):
        dq_out[pl.ds(h * HALF, HALF), :] = parts[h].astype(F32) + parts[2 + h].astype(F32)
    for copy in copies:
        copy.wait()


def on_device(queries, keys, values, out_cotangent):
    queries, keys, values, out_cotangent = (
        pltpu.with_memory_space_constraint(x, pltpu.HBM) for x in (queries, keys, values, out_cotangent)
    )
    anywhere = pl.BlockSpec(memory_space=pl.ANY)
    dma = pltpu.SemaphoreType.DMA
    parts, key_gradient, value_gradient = pl.pallas_call(
        kernel,
        out_shape=(
            pltpu.VMEM((DOCS, HALF, DH), BF16),
            pltpu.VMEM(keys.shape, BF16),
            pltpu.VMEM(values.shape, BF16),
        ),
        in_specs=[anywhere] * 4,
        out_specs=[pl.BlockSpec(memory_space=pltpu.VMEM)] * 3,
        scratch_shapes=[
            pltpu.VMEM((HERE, PAIR * DH), BF16),
            pltpu.VMEM((HERE, PAIR * DH), BF16),
            pltpu.VMEM((PAIR * R, DH), BF16),
            pltpu.VMEM((PAIR * R, DH), BF16),
            pltpu.VMEM((PAIR * CHUNKS, HERE, CHUNK), F32),
            pltpu.VMEM((PAIR * CHUNKS, HERE, CHUNK), F32),
            pltpu.VMEM((PAIR, HERE, R), BF16),
            pltpu.VMEM((PAIR, HERE, R), BF16),
            pltpu.VMEM((HERE, PAIR * DH), BF16),
            pltpu.VMEM((HERE, PAIR * DH), BF16),
            pltpu.VMEM((Z, BLOCK, DH), F32),
            pltpu.VMEM((Z, BLOCK, DH), BF16),
            pltpu.VMEM((Z, HALF, DH), BF16),
            pltpu.VMEM((Z, HALF, DH), BF16),
            pltpu.VMEM((Z, HALF, DH), BF16),
            pltpu.VMEM((PAIR, 1, R), F32),
            pltpu.VMEM((Z, 2 * PAIR, 1, R), F32),
            dma((4,)), dma((2,)), dma((2,)), dma((24,)), dma((24,)), dma((2,)), dma((2,)),
            dma((2,)), dma((2,)), dma((PAIR,)), dma((PAIR,)), dma((2,)), dma((2,)),
        ],
        compiler_params=pltpu.CompilerParams(
            collective_id=0, has_side_effects=True, vmem_limit_bytes=48 * 2**20
        ),
        cost_estimate=pl.CostEstimate(
            flops=10 * HERE * PAIR * R * DH, bytes_accessed=4 * 2**20, transcendentals=HERE * PAIR * R
        ),
    )(queries, keys, values, out_cotangent)
    return pl.pallas_call(
        finish,
        out_shape=(
            jax.ShapeDtypeStruct((BLOCK, DH), F32),
            jax.ShapeDtypeStruct(keys.shape, BF16),
            jax.ShapeDtypeStruct(values.shape, BF16),
        ),
        in_specs=[pl.BlockSpec(memory_space=pltpu.VMEM)] * 3,
        out_specs=(pl.BlockSpec(memory_space=pltpu.VMEM), anywhere, anywhere),
        scratch_shapes=[dma((2,))],
        compiler_params=pltpu.CompilerParams(vmem_limit_bytes=4 * 2**20),
    )(parts, key_gradient, value_gradient)


def solution(mesh):
    placed = (P("mp", None), P("dp", "mp", None), P("dp", "mp", None), P("dp", "mp", None))
    return jax.shard_map(
        on_device,
        mesh=mesh,
        in_specs=placed,
        out_specs=(P("mp", None), P("dp", "mp", None), P("dp", "mp", None)),
        check_vma=False,
    )
```

time: 63.7 us -> 53.9 us (0.85)
  local copies, waits for them, and re-layouts: 6.12 us -> 0 us
  Pallas kernels: 56.7 us -> 53.2 us
    unnamed x11 -> x0, local copies, waits for them, and re-layouts: 6.12 us -> none
    pallas_call x1 -> x2, Pallas kernels: 56.7 us -> 53.2 us  [the longest x1 51.6 us: on_device(): pl.pallas_call(kernel, out_shape=(pltpu.VMEM((DOCS, HALF, DH), BF16), plt...]
where the time goes in v2:
time: 53.9 us
  Pallas kernels  53.2 us (99%)
  between operations  0.64 us (1%)
    pallas_call x1, Pallas kernels, on_device(): pl.pallas_call(kernel, out_shape=(pltpu.VMEM((DOCS, HALF, DH), BF16), plt...  51.6 us
    pallas_call x1, Pallas kernels, on_device(): pl.pallas_call(finish, out_shape=(jax.ShapeDtypeStruct((BLOCK, DH), F32),...  1.66 us

profile of v2, /device:TPU:1, one launch (start us, length us, event | category | flops | bytes accessed | tf_op | source)
XLA Modules:
  0.0 53.9 jit_solution(16808322522376551971)
XLA Ops:
  0.6 51.6 %shard_map.67 = (bf16[4,96,256]{2,1,0:T(8,128)(2,1)S(1)}, bf16[1,64,4096]{2,1,0:T(8,128)(2,1)S(1)}, bf16[1,64,4096]{2,1,0:T(8,128)(2,1)S(1)}) custom-call(bf16[192,256]{1,0:T(8,128)(2,1)} %q_in.1, bf16[1,64,4096]{2,1,0:T(8,128)(2,1)} %k_in.1, bf16[1,64,4096]{2,1,0:T(8,128)(2,1)} %v_in.1, bf16[1,192,256]{2,1,0:T(8,128)(2,1)} %g_in.1), custom_call_target="tpu_custom_call" | custom-call | flops 2013265920 | bytes 4194304 | tf_op jit(solution)/shard_map/pallas_call | solution.py:293
  52.2 1.7 %shard_map.68 = (f32[192,256]{1,0:T(8,128)}, bf16[1,64,4096]{2,1,0:T(8,128)(2,1)}, bf16[1,64,4096]{2,1,0:T(8,128)(2,1)}) custom-call(bf16[4,96,256]{2,1,0:T(8,128)(2,1)S(1)} %get-tuple-element.6.parts, bf16[1,64,4096]{2,1,0:T(8,128)(2,1)S(1)} %get-tuple-element.7.dk_in, bf16[1,64,4096]{2,1,0:T(8,128)(2,1)S(1)} %get-tuple-element.8.dv_in), custom_call_target="tpu_custom_call" | custom-call | tf_op jit(solution)/shard_map/pallas_call | solution.py:330

commit v3 on v2

--- a/solution.py
+++ b/solution.py
@@ -19,8 +19,8 @@
 HALF = BLOCK // 2
 POS = 64
 HERE = K * POS
-CHUNK = 256
-CHUNKS = R // CHUNK
+WIDE = 2 * BLOCK
+WIDES = PAIR * R // WIDE
 SCALE = 1.0 / math.sqrt(DH)
 MESH = pl.DeviceIdType.MESH
 F32 = jnp.float32
@@ -34,9 +34,9 @@
 def kernel(
     q_in, k_in, v_in, g_in,
     yrecv, dk_out, dv_out,
-    kbuf, vbuf, qbuf, gbuf, pbuf, wbuf, p16, s16, dkst, dvst,
-    dq32, dq16, crecv, zsend, zrecv, mstat, stat,
-    own_sem, ksem, vsem, rsend, rrecv, shsem, stsem, dksem, dvsem, csend, crsem, zsem, ysem,
+    kbuf, vbuf, qbuf, gbuf, pbuf, wbuf, p16, s16, aq, bq, dkst, dvst,
+    dq32, dq16, crecv, zsend, zrecv, mstat, tstat, logs, deltas,
+    own_sem, ksem, vsem, rsend, rrecv, shsem, lsem, dsem, dksem, dvsem, csend, crsem, zsem, ysem,
 ):
     dp, mp = lax.axis_index("dp"), lax.axis_index("mp")
     k, z = lax.div(mp, Z), lax.rem(mp, Z)
@@ -63,10 +63,10 @@
         return j, (j, mp)
 
     barrier = pltpu.get_barrier_semaphore()
-    for others, count in ((mate, K), (ringmate, Z), (doc, DOCS)):
-        for d in range(1, count):
-            pl.semaphore_signal(barrier, inc=1, device_id=others(d)[1], device_id_type=MESH)
-    pl.semaphore_wait(barrier, K - 1 + Z - 1 + DOCS - 1)
+    partners = [mate(d)[1] for d in range(1, K)] + [doc(d)[1] for d in range(1, DOCS)] + [(dp, right), (dp, left)]
+    for where in partners:
+        pl.semaphore_signal(barrier, inc=1, device_id=where, device_id_type=MESH)
+    pl.semaphore_wait(barrier, len(partners))
 
     def rows_of(j, start, size):
         return pl.ds(pl.multiple_of(j * BLOCK + start, 16), size)
@@ -95,11 +95,11 @@
         j = lax.rem(z + (Z - 1 - h if side == 0 else h + 1), Z)
         start, size = (core * HALF, HALF) if h < 3 else (core * HALF + side * (HALF // 2), HALF // 2)
         there = qbuf.at[rows_of(j, start, size)]
-        return remote(there, there, shsem.at[0], shsem.at[1], (sibling, mp))
-
-    def shared():
-        there = qbuf.at[pl.ds(0, (Z - 1) * HALF)]
-        return remote(there, there, shsem.at[0], shsem.at[1], (sibling, mp))
+        return remote(there, there, shsem.at[0], shsem.at[1 + h // 3], (sibling, mp))
+
+    def shared(last):
+        there = qbuf.at[pl.ds(0, HALF if last else 6 * HALF)]
+        return remote(there, there, shsem.at[0], shsem.at[1 + last], (sibling, mp))
 
     for part in range(3):
         for side in range(2):
@@ -119,61 +119,99 @@
     for copy in own:
         copy.start()
 
-    for h in range(1, 5):
+    for h in range(1, 4):
         for part in range(3):
             for side in range(2):
-                if travels(part, h - 1, side):
-                    hop(part, h - 1, side).wait_recv()
-                    if h < 4 and travels(part, h, side):
-                        hop(part, h, side).start()
-                    if part == 0:
-                        share(h - 1, side).start()
+                hop(part, h - 1, side).wait_recv()
+                if travels(part, h, side):
+                    hop(part, h, side).start()
+                if part == 0:
+                    share(h - 1, side).start()
 
     def all_mates(buf, sem):
         there = buf.at[pl.ds(0, (K - 1) * POS)]
         return remote(there, there, sem.at[0], sem.at[1], mate(1)[1])
 
+    def place(w):
+        a = lax.div(w, 2)
+        head = pl.ds(pl.multiple_of(a * DH, DH), DH)
+        rows = pl.ds(pl.multiple_of(w * WIDE, WIDE), WIDE)
+        cols = pl.ds(pl.multiple_of(lax.rem(w, 2) * WIDE, WIDE), WIDE)
+        return a, head, rows, cols
+
+    def score(w):
+        a, head, rows, cols = place(w)
+        s = dot(kbuf[:, head], qbuf[rows, :], ((1,), (1,))) * SCALE
+        top = jnp.max(s, axis=0, keepdims=True)
+        p = jnp.exp(s - top)
+        total = jnp.sum(p, axis=0, keepdims=True)
+        pbuf[w] = p
+        p16[a, :, cols] = p.astype(BF16)
+        mstat[a, :, cols] = top
+        tstat[a, :, cols] = total
+        logs[z, a, :, cols] = top + jnp.log(total)
+
+    def weigh(w):
+        a, head, rows, cols = place(w)
+        c = dot(vbuf[:, head], gbuf[rows, :], ((1,), (1,)))
+        wbuf[w] = c
+        deltas[z, a, :, cols] = jnp.sum(pbuf[w] * c, axis=0, keepdims=True) / tstat[a, :, cols]
+
+    def settle(w):
+        a, head, rows, cols = place(w)
+        s16[a, :, cols] = (pbuf[w] * (wbuf[w] - deltas[z, a, :, cols])).astype(BF16)
+
+    pair = lax.div(z, 2)
+    early = [pair, lax.rem(pair + 1, WIDES), lax.rem(pair + 3, WIDES)]
+    late = lax.rem(pair + 2, WIDES)
     for copy in own:
         copy.wait()
-    shared().wait_recv()
+    shared(0).wait_recv()
     all_mates(kbuf, ksem).wait_recv()
+    for w in early:
+        score(w)
+    for side in range(2):
+        hop(0, 3, side).wait_recv()
+        share(3, side).start()
     all_mates(vbuf, vsem).wait_recv()
-
+    for w in early:
+        weigh(w)
+        settle(w)
+    def tell(stat, sem):
+        for d in (4, 3, 5, 2, 6, 1, 7):
+            remote(stat.at[z], stat.at[z], sem.at[0], sem.at[1], ringmate(d)[1]).start()
+
+    def told(stat, sem):
+        there = stat.at[pl.ds(0, Z - 1)]
+        return remote(there, there, sem.at[0], sem.at[1], ringmate(1)[1])
+
+    shared(1).wait_recv()
+    score(late)
+    tell(logs, lsem)
+    for side in range(2):
+        hop(side + 1, 3, side).wait_recv()
+    weigh(late)
+    tell(deltas, dsem)
+    settle(late)
     for a in range(PAIR):
-        head = pl.ds(a * DH, DH)
-        for c in range(CHUNKS):
-            i = a * CHUNKS + c
-            rows, cols = pl.ds(i * CHUNK, CHUNK), pl.ds(c * CHUNK, CHUNK)
-            s = dot(kbuf[:, head], qbuf[rows, :], ((1,), (1,))) * SCALE
-            top = jnp.max(s, axis=0, keepdims=True)
-            p = jnp.exp(s - top)
-            total = jnp.sum(p, axis=0, keepdims=True)
-            w = dot(vbuf[:, head], gbuf[rows, :], ((1,), (1,)))
-            delta = jnp.sum(p * w, axis=0, keepdims=True)
-            pbuf[i] = p
-            wbuf[i] = w
-            mstat[a, :, cols] = top
-            stat[z, 2 * a, :, cols] = top + jnp.log(total)
-            stat[z, 2 * a + 1, :, cols] = delta / total
-
-    for d in (4, 3, 5, 2, 6, 1, 7):
-        j, where = ringmate(d)
-        remote(stat.at[z], stat.at[z], stsem.at[0], stsem.at[1], where).start()
-
-    def all_stats():
-        there = stat.at[pl.ds(0, Z - 1)]
-        return remote(there, there, stsem.at[0], stsem.at[1], ringmate(1)[1])
-
-    all_stats().wait_recv()
-
-    def core_copy(a):
-        mine = pl.ds(pl.multiple_of((1 - core) * HALF, HALF), HALF)
-        there = pl.ds(a * (Z // 2), Z // 2)
-        return remote(dq16.at[there, mine], crecv.at[there], csend.at[a], crsem.at[a], (sibling, mp))
-
+        there = kbuf[:, a * DH : (a + 1) * DH]
+        aq[a] = dot(s16[a], there, ((0,), (0,)))
+        bq[a] = dot(p16[a], there, ((0,), (0,)))
+
+    def columns(rows):
+        return jnp.concatenate(rows + [jnp.zeros((8 - len(rows), R), F32)], axis=0).T
+
+    def back(stage, out, sem, values_of):
+        for a in range(PAIR):
+            stage[:, a * DH : (a + 1) * DH] = values_of(a).astype(BF16)
+        for d in range(1, K):
+            j, where = mate(d)
+            remote(stage.at[pos_of(j)], out.at[0, :, cols_of(k)], sem.at[0], sem.at[1], where).start()
+
+    told(logs, lsem).wait_recv()
+    weights, factors = [], []
     for a in range(PAIR):
-        head = pl.ds(a * DH, DH)
-        parts = [stat[j, 2 * a] for j in range(Z)]
+        parts = [logs[j, a] for j in range(Z)]
         peak = parts[0]
         for part in parts[1:]:
             peak = jnp.maximum(peak, part)
@@ -181,48 +219,67 @@
         whole = shares[0]
         for part in shares[1:]:
             whole = whole + part
-        delta = shares[0] * stat[0, 2 * a + 1]
+        weights.append([share / whole for share in shares])
+        factors.append(jnp.exp(mstat[a] - (peak + jnp.log(whole))))
+    factor = columns(factors)
+
+    def value_part(a):
+        rows = gbuf[pl.ds(a * R, R), :].astype(F32) * factor[:, a : a + 1]
+        return dot(p16[a], rows.astype(BF16), ((1,), (0,)))
+
+    back(dvst, dv_out, dvsem, value_part)
+
+    def core_copy(a):
+        mine = pl.ds(pl.multiple_of((1 - core) * HALF, HALF), HALF)
+        there = pl.ds(a * (Z // 2), Z // 2)
+        return remote(dq16.at[there, mine], crecv.at[there], csend.at[a], crsem.at[a], (sibling, mp))
+
+    told(deltas, dsem).wait_recv()
+    changes = []
+    for a in range(PAIR):
+        delta = weights[a][0] * deltas[0, a]
         for j in range(1, Z):
-            delta = delta + shares[j] * stat[j, 2 * a + 1]
-        delta = delta / whole
-        factor = jnp.exp(mstat[a] - (peak + jnp.log(whole)))
-        for c in range(CHUNKS):
-            i = a * CHUNKS + c
-            lo, hi = c * CHUNK, (c + 1) * CHUNK
-            p = pbuf[i] * factor[:, lo:hi]
-            p16[a, :, lo:hi] = p.astype(BF16)
-            s16[a, :, lo:hi] = (p * (wbuf[i] - delta[:, lo:hi])).astype(BF16)
+            delta = delta + weights[a][j] * deltas[j, a]
+        changes.append(factors[a] * (deltas[z, a] - delta))
+    change = columns(changes)
+
+    def query_part(a):
         there = pl.ds(a * (Z // 2), Z // 2)
-        part = (dot(s16[a], kbuf[:, head], ((0,), (0,))) * SCALE).reshape(Z // 2, BLOCK, DH)
+        part = (factor[:, a : a + 1] * aq[a] + change[:, a : a + 1] * bq[a]) * SCALE
+        part = part.reshape(Z // 2, BLOCK, DH)
         dq32[there] = part
         dq16[there] = part.astype(BF16)
         core_copy(a).start()
 
-    def back(stage, out, sem, values_of):
-        for a in range(PAIR):
-            stage[:, a * DH : (a + 1) * DH] = values_of(a).astype(BF16)
-        for d in range(1, K):
-            j, where = mate(d)
-            remote(stage.at[pos_of(j)], out.at[0, :, cols_of(k)], sem.at[0], sem.at[1], where).start()
-
-    back(dvst, dv_out, dvsem, lambda a: dot(p16[a], gbuf[pl.ds(a * R, R), :], ((1,), (0,))))
+    def key_part(a):
+        rows = qbuf[pl.ds(a * R, R), :].astype(F32)
+        main = (rows * (factor[:, a : a + 1] * SCALE)).astype(BF16)
+        rest = (rows * (change[:, a : a + 1] * SCALE)).astype(BF16)
+        return dot(s16[a], main, ((1,), (0,))) + dot(p16[a], rest, ((1,), (0,)))
 
     def z_copy(j):
         return remote(zsend.at[j], zrecv.at[z], zsem.at[0], zsem.at[1], (dp, k * Z + j))
 
-    for a in range(PAIR):
+    def over_z(a):
         core_copy(a).wait_recv()
-    for d in (4, 3, 5, 2, 6, 1, 7, 0):
-        j = lax.rem(z + d, Z)
         mine = pl.ds(pl.multiple_of(core * HALF, HALF), HALF)
-        part = (dq32[j, mine, :] + crecv[j].astype(F32)).astype(BF16)
-        if d:
-            zsend[j] = part
-            z_copy(j).start()
-        else:
-            zrecv[j] = part
-
-    back(dkst, dk_out, dksem, lambda a: dot(s16[a], qbuf[pl.ds(a * R, R), :], ((1,), (0,))) * SCALE)
+        for c in range(Z // 2):
+            j = a * (Z // 2) + lax.rem(z + 2 + c, Z // 2)
+            zsend[j] = (dq32[j, mine, :] + crecv[j].astype(F32)).astype(BF16)
+
+            @pl.when(j != z)
+            def _():
+                z_copy(j).start()
+
+            @pl.when(j == z)
+            def _():
+                zrecv[z] = zsend[z]
+
+    query_part(0)
+    query_part(1)
+    over_z(0)
+    over_z(1)
+    back(dkst, dk_out, dksem, key_part)
     kept = [
         pltpu.make_async_copy(dvst.at[pos_of(k)], dv_out.at[0, :, cols_of(k)], own_sem.at[0]),
         pltpu.make_async_copy(dkst.at[pos_of(k)], dk_out.at[0, :, cols_of(k)], own_sem.at[1]),
@@ -235,10 +292,12 @@
             for side in range(2):
                 if travels(part, h, side):
                     hop(part, h, side).wait_send()
-    shared().wait_send()
+    shared(0).wait_send()
+    shared(1).wait_send()
     all_mates(kbuf, ksem).wait_send()
     all_mates(vbuf, vsem).wait_send()
-    all_stats().wait_send()
+    told(logs, lsem).wait_send()
+    told(deltas, dsem).wait_send()
     for a in range(PAIR):
         core_copy(a).wait_send()
 
@@ -304,10 +363,12 @@
             pltpu.VMEM((HERE, PAIR * DH), BF16),
             pltpu.VMEM((PAIR * R, DH), BF16),
             pltpu.VMEM((PAIR * R, DH), BF16),
-            pltpu.VMEM((PAIR * CHUNKS, HERE, CHUNK), F32),
-            pltpu.VMEM((PAIR * CHUNKS, HERE, CHUNK), F32),
+            pltpu.VMEM((WIDES, HERE, WIDE), F32),
+            pltpu.VMEM((WIDES, HERE, WIDE), F32),
             pltpu.VMEM((PAIR, HERE, R), BF16),
             pltpu.VMEM((PAIR, HERE, R), BF16),
+            pltpu.VMEM((PAIR, R, DH), F32),
+            pltpu.VMEM((PAIR, R, DH), F32),
             pltpu.VMEM((HERE, PAIR * DH), BF16),
             pltpu.VMEM((HERE, PAIR * DH), BF16),
             pltpu.VMEM((Z, BLOCK, DH), F32),
@@ -316,8 +377,10 @@
             pltpu.VMEM((Z, HALF, DH), BF16),
             pltpu.VMEM((Z, HALF, DH), BF16),
             pltpu.VMEM((PAIR, 1, R), F32),
-            pltpu.VMEM((Z, 2 * PAIR, 1, R), F32),
-            dma((4,)), dma((2,)), dma((2,)), dma((24,)), dma((24,)), dma((2,)), dma((2,)),
+            pltpu.VMEM((PAIR, 1, R), F32),
+            pltpu.VMEM((Z, PAIR, 1, R), F32),
+            pltpu.VMEM((Z, PAIR, 1, R), F32),
+            dma((4,)), dma((2,)), dma((2,)), dma((24,)), dma((24,)), dma((3,)), dma((2,)), dma((2,)),
             dma((2,)), dma((2,)), dma((PAIR,)), dma((PAIR,)), dma((2,)), dma((2,)),
         ],
         compiler_params=pltpu.CompilerParams(

time: 53.9 us -> 51.6 us (0.957)
  Pallas kernels: 53.2 us -> 50.8 us
    pallas_call x1, Pallas kernels: 51.6 us -> 49.2 us  [on_device(): pl.pallas_call(kernel, out_shape=(pltpu.VMEM((DOCS, HALF, DH), BF16), plt...]
where the time goes in v3:
time: 51.6 us; the launch traced here: 51.5 us
  Pallas kernels  50.8 us (98%)
  between operations  0.64 us (1%)
    pallas_call x1, Pallas kernels, on_device(): pl.pallas_call(kernel, out_shape=(pltpu.VMEM((DOCS, HALF, DH), BF16), plt...  49.2 us
    pallas_call x1, Pallas kernels, on_device(): pl.pallas_call(finish, out_shape=(jax.ShapeDtypeStruct((BLOCK, DH), F32),...  1.66 us

profile of v3, /device:TPU:1, one launch (start us, length us, event | category | flops | bytes accessed | tf_op | source)
XLA Modules:
  0.0 51.5 jit_solution(10407086092848283919)
XLA Ops:
  0.6 49.2 %shard_map.67 = (bf16[4,96,256]{2,1,0:T(8,128)(2,1)S(1)}, bf16[1,64,4096]{2,1,0:T(8,128)(2,1)S(1)}, bf16[1,64,4096]{2,1,0:T(8,128)(2,1)S(1)}) custom-call(bf16[192,256]{1,0:T(8,128)(2,1)} %q_in.1, bf16[1,64,4096]{2,1,0:T(8,128)(2,1)} %k_in.1, bf16[1,64,4096]{2,1,0:T(8,128)(2,1)} %v_in.1, bf16[1,192,256]{2,1,0:T(8,128)(2,1)} %g_in.1), custom_call_target="tpu_custom_call" | custom-call | flops 2013265920 | bytes 4194304 | tf_op jit(solution)/shard_map/pallas_call | solution.py:352
  49.8 1.7 %shard_map.68 = (f32[192,256]{1,0:T(8,128)}, bf16[1,64,4096]{2,1,0:T(8,128)(2,1)}, bf16[1,64,4096]{2,1,0:T(8,128)(2,1)}) custom-call(bf16[4,96,256]{2,1,0:T(8,128)(2,1)S(1)} %get-tuple-element.6.parts, bf16[1,64,4096]{2,1,0:T(8,128)(2,1)S(1)} %get-tuple-element.7.dk_in, bf16[1,64,4096]{2,1,0:T(8,128)(2,1)S(1)} %get-tuple-element.8.dv_in), custom_call_target="tpu_custom_call" | custom-call | tf_op jit(solution)/shard_map/pallas_call | solution.py:393

commit v4 on v3

v4 whole, which is shorter than its diff:
```python
import math

import jax
import jax.numpy as jnp
from jax import lax
from jax.experimental import pallas as pl
from jax.experimental.pallas import tpu as pltpu
from jax.sharding import PartitionSpec as P

HEADS = 16
DH = 256
R = 768
DOCS = 4
MP = 64
CORES = 2
Z = 8
OWNERS = Z // 2
K = MP // Z
BLOCK = 192
HALF = BLOCK // 2
POS = 64
HERE = K * POS
WIDE = 2 * BLOCK
SCALE = 1.0 / math.sqrt(DH)
MESH = pl.DeviceIdType.MESH
F32 = jnp.float32
BF16 = jnp.bfloat16


def dot(a, b, dims):
    return lax.dot_general(a, b, (dims, ((), ())), preferred_element_type=F32)


def kernel(
    q_in, k_in, v_in, g_in,
    yrecv, dk_out, dv_out,
    kbuf, vbuf, qbuf, gbuf, pbuf, wbuf, p16, s16, aq, bq, dkst, dvst,
    zsend, zrecv, mstat, tstat, logs, deltas,
    own_sem, ksem, vsem, rsend, rrecv, gsem, lsem, dsem, dksem, dvsem, zsem, zown, ysem,
):
    dp, mp = lax.axis_index("dp"), lax.axis_index("mp")
    k, z = lax.div(mp, Z), lax.rem(mp, Z)
    core = lax.rem(dp, CORES)
    first_core = dp - core
    sibling = first_core + 1 - core
    home = lax.div(z, OWNERS)
    right = k * Z + lax.rem(z + 1, Z)
    left = k * Z + lax.rem(z + Z - 1, Z)

    def remote(src, dst, ssem, rsem, where):
        return pltpu.make_async_remote_copy(
            src_ref=src, dst_ref=dst, send_sem=ssem, recv_sem=rsem, device_id=where, device_id_type=MESH
        )

    def mate(d):
        j = lax.rem(k + d, K)
        return j, j * Z + z

    def ringmate(d):
        return dp, k * Z + lax.rem(z + d, Z)

    def doc(d):
        return lax.rem(dp + d, DOCS), mp

    barrier = pltpu.get_barrier_semaphore()
    partners = [(first_core + c, mate(d)[1]) for d in range(1, K) for c in range(CORES)]
    partners += [(sibling, right), (sibling, left)]
    partners += [ringmate(d) for d in range(1, Z)]
    partners += [doc(d) for d in range(1, DOCS)]
    for where in partners:
        pl.semaphore_signal(barrier, inc=1, device_id=where, device_id_type=MESH)
    pl.semaphore_wait(barrier, len(partners))

    def pos_of(j, which=0):
        return pl.ds(pl.multiple_of(which * HERE + j * POS, POS), POS)

    def cols_of(j, which):
        return pl.ds(pl.multiple_of((j * CORES + which) * DH, DH), DH)

    def piece(part, j, h, side):
        start = lax.rem(j, OWNERS) * BLOCK + (side * HALF if h == 3 else 0)
        size = HALF if h == 3 else BLOCK
        if part == 0:
            return qbuf.at[pl.ds(pl.multiple_of(start, 32), size)]
        return gbuf.at[pl.ds(pl.multiple_of((part - 1) * R + start, 32), size)]

    def own_cotangent():
        return gbuf.at[pl.ds(pl.multiple_of(core * R + lax.rem(z, OWNERS) * BLOCK, 32), BLOCK)]

    def slot(part, h, side):
        return (part * 2 + side) * 4 + h

    def hop(part, h, side):
        j = lax.rem(z + (Z - h if side == 0 else h), Z)
        there = piece(part, j, h, side)
        src = q_in if h == 0 else there
        i = slot(part, h, side)
        return remote(src, there, rsend.at[i], rrecv.at[i], (dp, right if side == 0 else left))

    def arrival(part, h, side):
        j = lax.rem(z + (Z - 1 - h if side == 0 else h + 1), Z)
        there = piece(part, j, h, side)
        i = slot(part, h, side)
        return remote(there, there, rsend.at[i], rrecv.at[i], (dp, right if side == 0 else left))

    def concerns(h, side):
        j = lax.rem(z + (Z - 1 - h if side == 0 else h + 1), Z)
        return lax.div(j, OWNERS) == core

    def cotangent_hop(side):
        where = (first_core + home, right if side == 0 else left)
        return remote(g_in.at[0], own_cotangent(), gsem.at[side], rrecv.at[4 * side + 8 + 8 * core], where)

    def cotangent_share():
        return remote(g_in.at[0], own_cotangent(), gsem.at[2], gsem.at[3], (sibling, mp))

    @pl.when(core == home)
    def _():
        for side in range(2):
            hop(0, 0, side).start()

    for side in range(2):
        cotangent_hop(side).start()

    @pl.when(core != home)
    def _():
        cotangent_share().start()

    def spread(src, buf, sem):
        for d in range(1, K):
            j, there = mate(d)
            for c in range(CORES):
                where = (first_core + c, there)
                remote(src.at[0, :, cols_of(j, c)], buf.at[pos_of(k, core)], sem.at[0], sem.at[1], where).start()
        where = (sibling, mp)
        remote(src.at[0, :, cols_of(k, 1 - core)], buf.at[pos_of(k, core)], sem.at[0], sem.at[1], where).start()

    spread(k_in, kbuf, ksem)
    spread(v_in, vbuf, vsem)

    own = [
        pltpu.make_async_copy(k_in.at[0, :, cols_of(k, core)], kbuf.at[pos_of(k, core)], own_sem.at[2]),
        pltpu.make_async_copy(v_in.at[0, :, cols_of(k, core)], vbuf.at[pos_of(k, core)], own_sem.at[3]),
    ]
    own_block = [
        pltpu.make_async_copy(q_in, piece(0, z, 0, 0), own_sem.at[0]),
        pltpu.make_async_copy(g_in.at[0], own_cotangent(), own_sem.at[1]),
    ]
    for copy in own:
        copy.start()

    @pl.when(core == home)
    def _():
        for copy in own_block:
            copy.start()

    for h in range(1, 4):
        for part in range(3):
            for side in range(2):

                @pl.when(concerns(h - 1, side))
                def _(h=h, part=part, side=side):
                    arrival(part, h - 1, side).wait_recv()
                    hop(part, h, side).start()

    def all_mates(buf, sem):
        there = buf.at[pl.ds(0, (CORES * K - 1) * POS)]
        return remote(there, there, sem.at[0], sem.at[1], (sibling, mp))

    def place(d, w):
        rows = pl.ds(pl.multiple_of(w * WIDE, WIDE), WIDE)
        cotangents = pl.ds(pl.multiple_of(d * R + w * WIDE, WIDE), WIDE)
        return d * 2 + w, pl.ds(d * HERE, HERE), rows, cotangents

    def score(d, w):
        i, docs, rows, _ = place(d, w)
        s = dot(kbuf[docs, :], qbuf[rows, :], ((1,), (1,))) * SCALE
        top = jnp.max(s, axis=0, keepdims=True)
        p = jnp.exp(s - top)
        total = jnp.sum(p, axis=0, keepdims=True)
        pbuf[i] = p
        p16[d, :, rows] = p.astype(BF16)
        mstat[d, :, rows] = top
        tstat[d, :, rows] = total
        logs[z, d, :, rows] = top + jnp.log(total)

    def weigh(d, w):
        i, docs, rows, cotangents = place(d, w)
        c = dot(vbuf[docs, :], gbuf[cotangents, :], ((1,), (1,)))
        wbuf[i] = c
        deltas[z, d, :, rows] = jnp.sum(pbuf[i] * c, axis=0, keepdims=True) / tstat[d, :, rows]

    def settle(d, w):
        i, _, rows, _ = place(d, w)
        s16[d, :, rows] = (pbuf[i] * (wbuf[i] - deltas[z, d, :, rows])).astype(BF16)

    late = lax.div(lax.rem(z, OWNERS), 2)
    early = 1 - late
    for copy in own:
        copy.wait()

    @pl.when(core == home)
    def _():
        for copy in own_block:
            copy.wait()
        cotangent_share().wait_recv()

    all_mates(kbuf, ksem).wait_recv()
    for d in range(CORES):
        score(d, early)
    all_mates(vbuf, vsem).wait_recv()
    for d in range(CORES):
        weigh(d, early)
        settle(d, early)

    def last(part):
        @pl.when(core != home)
        def _():
            for side in range(2):
                arrival(part, 3, side).wait_recv()

    def tell(stat, sem):
        for d in (4, 3, 5, 2, 6, 1, 7):
            remote(stat.at[z], stat.at[z], sem.at[0], sem.at[1], ringmate(d)).start()

    def told(stat, sem):
        there = stat.at[pl.ds(0, Z - 1)]
        return remote(there, there, sem.at[0], sem.at[1], ringmate(1))

    last(0)
    for d in range(CORES):
        score(d, late)
    tell(logs, lsem)
    for d in range(CORES):
        last(1 + d)
        weigh(d, late)
    tell(deltas, dsem)
    for d in range(CORES):
        docs = pl.ds(d * HERE, HERE)
        settle(d, late)
        aq[d] = dot(s16[d], kbuf[docs, :], ((0,), (0,)))
        bq[d] = dot(p16[d], kbuf[docs, :], ((0,), (0,)))

    def columns(rows):
        return jnp.concatenate(rows + [jnp.zeros((8 - len(rows), R), F32)], axis=0).T

    def back(stage, out, sem, values_of):
        for d in range(CORES):
            stage[d * HERE : (d + 1) * HERE, :] = values_of(d).astype(BF16)
        there = out.at[0, :, cols_of(k, core)]
        for e in range(1, K):
            j, to = mate(e)
            for d in range(CORES):
                remote(stage.at[pos_of(j, d)], there, sem.at[0], sem.at[1], (first_core + d, to)).start()
        remote(stage.at[pos_of(k, 1 - core)], there, sem.at[0], sem.at[1], (sibling, mp)).start()

    told(logs, lsem).wait_recv()
    weights, factors = [], []
    for d in range(CORES):
        parts = [logs[j, d] for j in range(Z)]
        peak = parts[0]
        for part in parts[1:]:
            peak = jnp.maximum(peak, part)
        shares = [jnp.exp(part - peak) for part in parts]
        whole = shares[0]
        for part in shares[1:]:
            whole = whole + part
        weights.append([share / whole for share in shares])
        factors.append(jnp.exp(mstat[d] - (peak + jnp.log(whole))))
    factor = columns(factors)

    def value_part(d):
        rows = gbuf[d * R : (d + 1) * R, :].astype(F32) * factor[:, d : d + 1]
        return dot(p16[d], rows.astype(BF16), ((1,), (0,)))

    back(dvst, dv_out, dvsem, value_part)

    told(deltas, dsem).wait_recv()
    changes = []
    for d in range(CORES):
        delta = weights[d][0] * deltas[0, d]
        for j in range(1, Z):
            delta = delta + weights[d][j] * deltas[j, d]
        changes.append(factors[d] * (deltas[z, d] - delta))
    change = columns(changes)

    def z_copy(b, c):
        src = zsend.at[b, pl.ds(c * HALF, HALF)]
        where = (first_core + c, k * Z + core * OWNERS + b)
        return remote(src, zrecv.at[z], zsem.at[0], zsem.at[1], where)

    def z_own():
        src = zsend.at[lax.rem(z, OWNERS), pl.ds(pl.multiple_of((1 - core) * HALF, HALF), HALF)]
        return remote(src, zrecv.at[z], zown.at[0], zown.at[1], (sibling, mp))

    for b in range(OWNERS):
        rows = slice(b * BLOCK, (b + 1) * BLOCK)
        part = factor[rows, 0:1] * aq[0, rows, :] + change[rows, 0:1] * bq[0, rows, :]
        part = part + factor[rows, 1:2] * aq[1, rows, :] + change[rows, 1:2] * bq[1, rows, :]
        zsend[b] = (part * SCALE).astype(BF16)

        @pl.when(core * OWNERS + b != z)
        def _(b=b):
            for c in range(CORES):
                z_copy(b, c).start()

    @pl.when(core == home)
    def _():
        z_own().start()
        mine = pl.ds(pl.multiple_of(core * HALF, HALF), HALF)
        zrecv[z] = zsend[lax.rem(z, OWNERS), mine, :]

    def key_part(d):
        rows = qbuf[...].astype(F32)
        main = (rows * (factor[:, d : d + 1] * SCALE)).astype(BF16)
        rest = (rows * (change[:, d : d + 1] * SCALE)).astype(BF16)
        return dot(s16[d], main, ((1,), (0,))) + dot(p16[d], rest, ((1,), (0,)))

    back(dkst, dk_out, dksem, key_part)
    kept = [
        pltpu.make_async_copy(dvst.at[pos_of(k, core)], dv_out.at[0, :, cols_of(k, core)], own_sem.at[0]),
        pltpu.make_async_copy(dkst.at[pos_of(k, core)], dk_out.at[0, :, cols_of(k, core)], own_sem.at[1]),
    ]
    for copy in kept:
        copy.start()

    @pl.when(core == home)
    def _():
        for side in range(2):
            hop(0, 0, side).wait_send()

    for side in range(2):
        cotangent_hop(side).wait_send()

    @pl.when(core != home)
    def _():
        cotangent_share().wait_send()

    for h in range(1, 4):
        for side in range(2):

            @pl.when(concerns(h - 1, side))
            def _(h=h, side=side):
                for part in range(3):
                    hop(part, h, side).wait_send()

    all_mates(kbuf, ksem).wait_send()
    all_mates(vbuf, vsem).wait_send()
    told(logs, lsem).wait_send()
    told(deltas, dsem).wait_send()

    @pl.when(core != home)
    def _():
        z_own().wait_recv()

    pieces = zrecv.at[pl.ds(0, Z - 1)]
    remote(pieces, pieces, zsem.at[0], zsem.at[1], ringmate(1)).wait_recv()
    half_sum = zrecv[0].astype(F32)
    for j in range(1, Z):
        half_sum = half_sum + zrecv[j].astype(F32)
    yrecv[dp] = half_sum.astype(BF16)

    for d in range(1, DOCS):
        remote(yrecv.at[dp], yrecv.at[dp], ysem.at[0], ysem.at[1], doc(d)).start()

    def all_docs():
        there = yrecv.at[pl.ds(0, DOCS - 1)]
        return remote(there, there, ysem.at[0], ysem.at[1], doc(1))

    all_docs().wait_recv()
    for copy in kept:
        copy.wait()
    for out, sem in ((dv_out, dvsem), (dk_out, dksem)):
        there = out.at[0, :, pl.ds(0, (CORES * K - 1) * DH)]
        done = remote(there, there, sem.at[0], sem.at[1], (sibling, mp))
        done.wait_send()
        done.wait_recv()

    @pl.when(core == home)
    def _():
        z_own().wait_send()

    for b in range(OWNERS):

        @pl.when(core * OWNERS + b != z)
        def _(b=b):
            for c in range(CORES):
                z_copy(b, c).wait_send()

    all_docs().wait_send()


def finish(parts, dk_in, dv_in, dq_out, dk_out, dv_out, sem):
    copies = [
        pltpu.make_async_copy(dk_in, dk_out, sem.at[0]),
        pltpu.make_async_copy(dv_in, dv_out, sem.at[1]),
    ]
    for copy in copies:
        copy.start()
    for h in range(2):
        dq_out[pl.ds(h * HALF, HALF), :] = parts[h].astype(F32) + parts[2 + h].astype(F32)
    for copy in copies:
        copy.wait()


def on_device(queries, keys, values, out_cotangent):
    queries, keys, values, out_cotangent = (
        pltpu.with_memory_space_constraint(x, pltpu.HBM) for x in (queries, keys, values, out_cotangent)
    )
    anywhere = pl.BlockSpec(memory_space=pl.ANY)
    inside = pl.BlockSpec(memory_space=pltpu.VMEM)
    dma = pltpu.SemaphoreType.DMA
    parts, key_gradient, value_gradient = pl.pallas_call(
        kernel,
        out_shape=(
            pltpu.VMEM((DOCS, HALF, DH), BF16),
            pltpu.VMEM(keys.shape, BF16),
            pltpu.VMEM(values.shape, BF16),
        ),
        in_specs=[anywhere] * 4,
        out_specs=[inside] * 3,
        scratch_shapes=[
            pltpu.VMEM((CORES * HERE, DH), BF16),
            pltpu.VMEM((CORES * HERE, DH), BF16),
            pltpu.VMEM((R, DH), BF16),
            pltpu.VMEM((CORES * R, DH), BF16),
            pltpu.VMEM((2 * CORES, HERE, WIDE), F32),
            pltpu.VMEM((2 * CORES, HERE, WIDE), F32),
            pltpu.VMEM((CORES, HERE, R), BF16),
            pltpu.VMEM((CORES, HERE, R), BF16),
            pltpu.VMEM((CORES, R, DH), F32),
            pltpu.VMEM((CORES, R, DH), F32),
            pltpu.VMEM((CORES * HERE, DH), BF16),
            pltpu.VMEM((CORES * HERE, DH), BF16),
            pltpu.VMEM((OWNERS, BLOCK, DH), BF16),
            pltpu.VMEM((Z, HALF, DH), BF16),
            pltpu.VMEM((CORES, 1, R), F32),
            pltpu.VMEM((CORES, 1, R), F32),
            pltpu.VMEM((Z, CORES, 1, R), F32),
            pltpu.VMEM((Z, CORES, 1, R), F32),
            dma((4,)), dma((2,)), dma((2,)), dma((24,)), dma((24,)), dma((4,)), dma((2,)), dma((2,)),
            dma((2,)), dma((2,)), dma((2,)), dma((2,)), dma((2,)),
        ],
        compiler_params=pltpu.CompilerParams(
            collective_id=0, has_side_effects=True, vmem_limit_bytes=48 * 2**20
        ),
        cost_estimate=pl.CostEstimate(
            flops=10 * HERE * CORES * R * DH, bytes_accessed=4 * 2**20, transcendentals=HERE * CORES * R
        ),
    )(queries, keys, values, out_cotangent)
    return pl.pallas_call(
        finish,
        out_shape=(
            jax.ShapeDtypeStruct((BLOCK, DH), F32),
            jax.ShapeDtypeStruct(keys.shape, BF16),
            jax.ShapeDtypeStruct(values.shape, BF16),
        ),
        in_specs=[inside] * 3,
        out_specs=(inside, anywhere, anywhere),
        scratch_shapes=[dma((2,))],
        compiler_params=pltpu.CompilerParams(vmem_limit_bytes=4 * 2**20),
    )(parts, key_gradient, value_gradient)


def solution(mesh):
    placed = (P("mp", None), P("dp", "mp", None), P("dp", "mp", None), P("dp", "mp", None))
    return jax.shard_map(
        on_device,
        mesh=mesh,
        in_specs=placed,
        out_specs=(P("mp", None), P("dp", "mp", None), P("dp", "mp", None)),
        check_vma=False,
    )
```

time: 51.6 us -> 50.6 us (0.981)
  Pallas kernels: 50.8 us -> 49.9 us
    pallas_call x1, Pallas kernels: 49.2 us -> 48.2 us  [on_device(): pl.pallas_call(kernel, out_shape=(pltpu.VMEM((DOCS, HALF, DH), BF16), plt...]
where the time goes in v4:
time: 50.6 us; the launch traced here: 50.5 us
  Pallas kernels  49.9 us (99%)
  between operations  0.64 us (1%)
    pallas_call x1, Pallas kernels, on_device(): pl.pallas_call(kernel, out_shape=(pltpu.VMEM((DOCS, HALF, DH), BF16), plt...  48.2 us
    pallas_call x1, Pallas kernels, on_device(): pl.pallas_call(finish, out_shape=(jax.ShapeDtypeStruct((BLOCK, DH), F32),...  1.66 us

profile of v4, /device:TPU:1, one launch (start us, length us, event | category | flops | bytes accessed | tf_op | source)
XLA Modules:
  0.0 50.5 jit_solution(5777899272149307783)
XLA Ops:
  0.6 48.2 %shard_map.67 = (bf16[4,96,256]{2,1,0:T(8,128)(2,1)S(1)}, bf16[1,64,4096]{2,1,0:T(8,128)(2,1)S(1)}, bf16[1,64,4096]{2,1,0:T(8,128)(2,1)S(1)}) custom-call(bf16[192,256]{1,0:T(8,128)(2,1)} %q_in.1, bf16[1,64,4096]{2,1,0:T(8,128)(2,1)} %k_in.1, bf16[1,64,4096]{2,1,0:T(8,128)(2,1)} %v_in.1, bf16[1,192,256]{2,1,0:T(8,128)(2,1)} %g_in.1), custom_call_target="tpu_custom_call" | custom-call | flops 2013265920 | bytes 4194304 | tf_op jit(solution)/shard_map/pallas_call | solution.py:413
  48.9 1.7 %shard_map.68 = (f32[192,256]{1,0:T(8,128)}, bf16[1,64,4096]{2,1,0:T(8,128)(2,1)}, bf16[1,64,4096]{2,1,0:T(8,128)(2,1)}) custom-call(bf16[4,96,256]{2,1,0:T(8,128)(2,1)S(1)} %get-tuple-element.6.parts, bf16[1,64,4096]{2,1,0:T(8,128)(2,1)S(1)} %get-tuple-element.7.dk_in, bf16[1,64,4096]{2,1,0:T(8,128)(2,1)S(1)} %get-tuple-element.8.dv_in), custom_call_target="tpu_custom_call" | custom-call | tf_op jit(solution)/shard_map/pallas_call | solution.py:451

commit v5 on v4

--- a/solution.py
+++ b/solution.py
@@ -34,7 +34,7 @@
 def kernel(
     q_in, k_in, v_in, g_in,
     yrecv, dk_out, dv_out,
-    kbuf, vbuf, qbuf, gbuf, pbuf, wbuf, p16, s16, aq, bq, dkst, dvst,
+    kown, vown, gown, kbuf, vbuf, qbuf, gbuf, pbuf, wbuf, p16, s16, aq, bq, dkst, dvst,
     zsend, zrecv, mstat, tstat, logs, deltas,
     own_sem, ksem, vsem, rsend, rrecv, gsem, lsem, dsem, dksem, dvsem, zsem, zown, ysem,
 ):
@@ -69,7 +69,6 @@
     partners += [doc(d) for d in range(1, DOCS)]
     for where in partners:
         pl.semaphore_signal(barrier, inc=1, device_id=where, device_id_type=MESH)
-    pl.semaphore_wait(barrier, len(partners))
 
     def pos_of(j, which=0):
         return pl.ds(pl.multiple_of(which * HERE + j * POS, POS), POS)
@@ -84,6 +83,9 @@
             return qbuf.at[pl.ds(pl.multiple_of(start, 32), size)]
         return gbuf.at[pl.ds(pl.multiple_of((part - 1) * R + start, 32), size)]
 
+    def own_queries():
+        return qbuf.at[pl.ds(pl.multiple_of(lax.rem(z, OWNERS) * BLOCK, 32), BLOCK)]
+
     def own_cotangent():
         return gbuf.at[pl.ds(pl.multiple_of(core * R + lax.rem(z, OWNERS) * BLOCK, 32), BLOCK)]
 
@@ -93,7 +95,7 @@
     def hop(part, h, side):
         j = lax.rem(z + (Z - h if side == 0 else h), Z)
         there = piece(part, j, h, side)
-        src = q_in if h == 0 else there
+        src = own_queries() if h == 0 else there
         i = slot(part, h, side)
         return remote(src, there, rsend.at[i], rrecv.at[i], (dp, right if side == 0 else left))
 
@@ -109,10 +111,34 @@
 
     def cotangent_hop(side):
         where = (first_core + home, right if side == 0 else left)
-        return remote(g_in.at[0], own_cotangent(), gsem.at[side], rrecv.at[4 * side + 8 + 8 * core], where)
+        return remote(gown, own_cotangent(), gsem.at[side], rrecv.at[4 * side + 8 + 8 * core], where)
 
     def cotangent_share():
-        return remote(g_in.at[0], own_cotangent(), gsem.at[2], gsem.at[3], (sibling, mp))
+        return remote(gown, own_cotangent(), gsem.at[2], gsem.at[3], (sibling, mp))
+
+    staged = [
+        pltpu.make_async_copy(q_in, own_queries(), own_sem.at[0]),
+        pltpu.make_async_copy(g_in.at[0], gown, own_sem.at[1]),
+        pltpu.make_async_copy(k_in.at[0], kown, own_sem.at[2]),
+        pltpu.make_async_copy(v_in.at[0], vown, own_sem.at[3]),
+    ]
+    own = [
+        pltpu.make_async_copy(gown, own_cotangent(), own_sem.at[1]),
+        pltpu.make_async_copy(kown.at[:, cols_of(k, core)], kbuf.at[pos_of(k, core)], own_sem.at[2]),
+        pltpu.make_async_copy(vown.at[:, cols_of(k, core)], vbuf.at[pos_of(k, core)], own_sem.at[3]),
+    ]
+
+    for copy in staged[1:]:
+        copy.start()
+
+    @pl.when(core == home)
+    def _():
+        staged[0].start()
+        staged[0].wait()
+
+    for copy in staged[1:]:
+        copy.wait()
+    pl.semaphore_wait(barrier, len(partners))
 
     @pl.when(core == home)
     def _():
@@ -127,32 +153,27 @@
         cotangent_share().start()
 
     def spread(src, buf, sem):
-        for d in range(1, K):
-            j, there = mate(d)
-            for c in range(CORES):
+        for other in range(CORES):
+            c = lax.rem(core + other, CORES)
+
+            @pl.loop(1, K)
+            def _(d):
+                j, there = mate(d)
                 where = (first_core + c, there)
-                remote(src.at[0, :, cols_of(j, c)], buf.at[pos_of(k, core)], sem.at[0], sem.at[1], where).start()
+                remote(src.at[:, cols_of(j, c)], buf.at[pos_of(k, core)], sem.at[0], sem.at[1], where).start()
+
         where = (sibling, mp)
-        remote(src.at[0, :, cols_of(k, 1 - core)], buf.at[pos_of(k, core)], sem.at[0], sem.at[1], where).start()
-
-    spread(k_in, kbuf, ksem)
-    spread(v_in, vbuf, vsem)
-
-    own = [
-        pltpu.make_async_copy(k_in.at[0, :, cols_of(k, core)], kbuf.at[pos_of(k, core)], own_sem.at[2]),
-        pltpu.make_async_copy(v_in.at[0, :, cols_of(k, core)], vbuf.at[pos_of(k, core)], own_sem.at[3]),
-    ]
-    own_block = [
-        pltpu.make_async_copy(q_in, piece(0, z, 0, 0), own_sem.at[0]),
-        pltpu.make_async_copy(g_in.at[0], own_cotangent(), own_sem.at[1]),
-    ]
-    for copy in own:
+        remote(src.at[:, cols_of(k, 1 - core)], buf.at[pos_of(k, core)], sem.at[0], sem.at[1], where).start()
+
+    spread(kown, kbuf, ksem)
+    spread(vown, vbuf, vsem)
+    for copy in own[1:]:
         copy.start()
 
     @pl.when(core == home)
     def _():
-        for copy in own_block:
-            copy.start()
+        own[0].start()
+
 
     for h in range(1, 4):
         for part in range(3):
@@ -196,13 +217,12 @@
 
     late = lax.div(lax.rem(z, OWNERS), 2)
     early = 1 - late
-    for copy in own:
+    for copy in own[1:]:
         copy.wait()
 
     @pl.when(core == home)
     def _():
-        for copy in own_block:
-            copy.wait()
+        own[0].wait()
         cotangent_share().wait_recv()
 
     all_mates(kbuf, ksem).wait_recv()
@@ -244,15 +264,18 @@
     def columns(rows):
         return jnp.concatenate(rows + [jnp.zeros((8 - len(rows), R), F32)], axis=0).T
 
-    def back(stage, out, sem, values_of):
-        for d in range(CORES):
-            stage[d * HERE : (d + 1) * HERE, :] = values_of(d).astype(BF16)
+    def back(stage, out, sem, d, values):
+        stage[d * HERE : (d + 1) * HERE, :] = values.astype(BF16)
         there = out.at[0, :, cols_of(k, core)]
-        for e in range(1, K):
+
+        @pl.loop(1, K)
+        def _(e):
             j, to = mate(e)
-            for d in range(CORES):
-                remote(stage.at[pos_of(j, d)], there, sem.at[0], sem.at[1], (first_core + d, to)).start()
-        remote(stage.at[pos_of(k, 1 - core)], there, sem.at[0], sem.at[1], (sibling, mp)).start()
+            remote(stage.at[pos_of(j, d)], there, sem.at[0], sem.at[1], (first_core + d, to)).start()
+
+        @pl.when(core != d)
+        def _():
+            remote(stage.at[pos_of(k, d)], there, sem.at[0], sem.at[1], (sibling, mp)).start()
 
     told(logs, lsem).wait_recv()
     weights, factors = [], []
@@ -273,7 +296,9 @@
         rows = gbuf[d * R : (d + 1) * R, :].astype(F32) * factor[:, d : d + 1]
         return dot(p16[d], rows.astype(BF16), ((1,), (0,)))
 
-    back(dvst, dv_out, dvsem, value_part)
+    back(dvst, dv_out, dvsem, 0, value_part(0))
+
+    aq[0] = factor[:, 0:1] * aq[0] + factor[:, 1:2] * aq[1]
 
     told(deltas, dsem).wait_recv()
     changes = []
@@ -295,8 +320,7 @@
 
     for b in range(OWNERS):
         rows = slice(b * BLOCK, (b + 1) * BLOCK)
-        part = factor[rows, 0:1] * aq[0, rows, :] + change[rows, 0:1] * bq[0, rows, :]
-        part = part + factor[rows, 1:2] * aq[1, rows, :] + change[rows, 1:2] * bq[1, rows, :]
+        part = aq[0, rows, :] + change[rows, 0:1] * bq[0, rows, :] + change[rows, 1:2] * bq[1, rows, :]
         zsend[b] = (part * SCALE).astype(BF16)
 
         @pl.when(core * OWNERS + b != z)
@@ -316,7 +340,9 @@
         rest = (rows * (change[:, d : d + 1] * SCALE)).astype(BF16)
         return dot(s16[d], main, ((1,), (0,))) + dot(p16[d], rest, ((1,), (0,)))
 
-    back(dkst, dk_out, dksem, key_part)
+    back(dvst, dv_out, dvsem, 1, value_part(1))
+    for d in range(CORES):
+        back(dkst, dk_out, dksem, d, key_part(d))
     kept = [
         pltpu.make_async_copy(dvst.at[pos_of(k, core)], dv_out.at[0, :, cols_of(k, core)], own_sem.at[0]),
         pltpu.make_async_copy(dkst.at[pos_of(k, core)], dk_out.at[0, :, cols_of(k, core)], own_sem.at[1]),
@@ -390,7 +416,7 @@
     all_docs().wait_send()
 
 
-def finish(parts, dk_in, dv_in, dq_out, dk_out, dv_out, sem):
+def finish(parts, dk_in, dv_in, dq_out, dk_out, dv_out, total, sem):
     copies = [
         pltpu.make_async_copy(dk_in, dk_out, sem.at[0]),
         pltpu.make_async_copy(dv_in, dv_out, sem.at[1]),
@@ -398,7 +424,9 @@
     for copy in copies:
         copy.start()
     for h in range(2):
-        dq_out[pl.ds(h * HALF, HALF), :] = parts[h].astype(F32) + parts[2 + h].astype(F32)
+        total[pl.ds(h * HALF, HALF), :] = parts[h].astype(F32) + parts[2 + h].astype(F32)
+    copies.append(pltpu.make_async_copy(total, dq_out, sem.at[2]))
+    copies[2].start()
     for copy in copies:
         copy.wait()
 
@@ -420,6 +448,9 @@
         in_specs=[anywhere] * 4,
         out_specs=[inside] * 3,
         scratch_shapes=[
+            pltpu.VMEM((POS, HEADS * DH), BF16),
+            pltpu.VMEM((POS, HEADS * DH), BF16),
+            pltpu.VMEM((BLOCK, DH), BF16),
             pltpu.VMEM((CORES * HERE, DH), BF16),
             pltpu.VMEM((CORES * HERE, DH), BF16),
             pltpu.VMEM((R, DH), BF16),
@@ -456,8 +487,8 @@
             jax.ShapeDtypeStruct(values.shape, BF16),
         ),
         in_specs=[inside] * 3,
-        out_specs=(inside, anywhere, anywhere),
-        scratch_shapes=[dma((2,))],
+        out_specs=[anywhere] * 3,
+        scratch_shapes=[pltpu.VMEM((BLOCK, DH), F32), dma((3,))],
         compiler_params=pltpu.CompilerParams(vmem_limit_bytes=4 * 2**20),
     )(parts, key_gradient, value_gradient)
 

time: 50.6 us -> 49.3 us (0.974)
  Pallas kernels: 49.9 us -> 48.5 us
    pallas_call x1, Pallas kernels: 48.2 us -> 47.5 us  [on_device(): pl.pallas_call(kernel, out_shape=(pltpu.VMEM((DOCS, HALF, DH), BF16), plt...]
    pallas_call x1, Pallas kernels: 1.66 us -> 1.05 us  [on_device(): pl.pallas_call(finish, out_shape=(jax.ShapeDtypeStruct((BLOCK, DH), F32),...]
where the time goes in v5:
time: 49.3 us; the launch traced here: 49.2 us
  Pallas kernels  48.5 us (98%)
  between operations  0.64 us (1%)
    pallas_call x1, Pallas kernels, on_device(): pl.pallas_call(kernel, out_shape=(pltpu.VMEM((DOCS, HALF, DH), BF16), plt...  47.5 us
    pallas_call x1, Pallas kernels, on_device(): pl.pallas_call(finish, out_shape=(jax.ShapeDtypeStruct((BLOCK, DH), F32),...  1.05 us

profile of v5, /device:TPU:1, one launch (start us, length us, event | category | flops | bytes accessed | tf_op | source)
XLA Modules:
  0.0 49.2 jit_solution(14982945920902315500)
XLA Ops:
  0.6 47.5 %shard_map.67 = (bf16[4,96,256]{2,1,0:T(8,128)(2,1)S(1)}, bf16[1,64,4096]{2,1,0:T(8,128)(2,1)S(1)}, bf16[1,64,4096]{2,1,0:T(8,128)(2,1)S(1)}) custom-call(bf16[192,256]{1,0:T(8,128)(2,1)} %q_in.1, bf16[1,64,4096]{2,1,0:T(8,128)(2,1)} %k_in.1, bf16[1,64,4096]{2,1,0:T(8,128)(2,1)} %v_in.1, bf16[1,192,256]{2,1,0:T(8,128)(2,1)} %g_in.1), custom_call_target="tpu_custom_call" | custom-call | flops 2013265920 | bytes 4194304 | tf_op jit(solution)/shard_map/pallas_call | solution.py:441
  48.1 1.1 %shard_map.68 = (f32[192,256]{1,0:T(8,128)}, bf16[1,64,4096]{2,1,0:T(8,128)(2,1)}, bf16[1,64,4096]{2,1,0:T(8,128)(2,1)}) custom-call(bf16[4,96,256]{2,1,0:T(8,128)(2,1)S(1)} %get-tuple-element.6.parts, bf16[1,64,4096]{2,1,0:T(8,128)(2,1)S(1)} %get-tuple-element.7.dk_in, bf16[1,64,4096]{2,1,0:T(8,128)(2,1)S(1)} %get-tuple-element.8.dv_in), custom_call_target="tpu_custom_call" | custom-call | tf_op jit(solution)/shard_map/pallas_call | solution.py:482

commit v6 on v5

--- a/solution.py
+++ b/solution.py
@@ -56,6 +56,12 @@
         j = lax.rem(k + d, K)
         return j, j * Z + z
 
+    def far_mate(e):
+        i, x, y = lax.rem(e, 4), lax.div(k, 2), lax.rem(k, 2)
+        dx = 2 + 3 * i + 3 * lax.div(i, 2) + 2 * lax.div(i, 3)
+        j = lax.rem(x + dx, 4) * 2 + lax.rem(y + 1 - lax.div(e, 4), 2)
+        return j, j * Z + z
+
     def ringmate(d):
         return dp, k * Z + lax.rem(z + d, Z)
 
@@ -153,14 +159,13 @@
         cotangent_share().start()
 
     def spread(src, buf, sem):
-        for other in range(CORES):
-            c = lax.rem(core + other, CORES)
-
-            @pl.loop(1, K)
-            def _(d):
-                j, there = mate(d)
+        @pl.loop(0, K - 1)
+        def _(e):
+            j, there = far_mate(e)
+            for c in range(CORES):
                 where = (first_core + c, there)
                 remote(src.at[:, cols_of(j, c)], buf.at[pos_of(k, core)], sem.at[0], sem.at[1], where).start()
+
 
         where = (sibling, mp)
         remote(src.at[:, cols_of(k, 1 - core)], buf.at[pos_of(k, core)], sem.at[0], sem.at[1], where).start()
@@ -268,9 +273,9 @@
         stage[d * HERE : (d + 1) * HERE, :] = values.astype(BF16)
         there = out.at[0, :, cols_of(k, core)]
 
-        @pl.loop(1, K)
+        @pl.loop(0, K - 1)
         def _(e):
-            j, to = mate(e)
+            j, to = far_mate(e)
             remote(stage.at[pos_of(j, d)], there, sem.at[0], sem.at[1], (first_core + d, to)).start()
 
         @pl.when(core != d)

time: 49.3 us -> 48.9 us (level); the launches traced: 49.2 us -> 48.1 us
  Pallas kernels: 48.5 us -> 47.5 us
    pallas_call x1, Pallas kernels: 47.5 us -> 46.4 us  [on_device(): pl.pallas_call(kernel, out_shape=(pltpu.VMEM((DOCS, HALF, DH), BF16), plt...]
where the time goes in v6:
time: 48.9 us; the launch traced here: 48.1 us
  Pallas kernels  47.5 us (97%)
  between operations  0.64 us (1%)
    pallas_call x1, Pallas kernels, on_device(): pl.pallas_call(kernel, out_shape=(pltpu.VMEM((DOCS, HALF, DH), BF16), plt...  46.4 us
    pallas_call x1, Pallas kernels, on_device(): pl.pallas_call(finish, out_shape=(jax.ShapeDtypeStruct((BLOCK, DH), F32),...  1.05 us

profile of v6, /device:TPU:1, one launch (start us, length us, event | category | flops | bytes accessed | tf_op | source)
XLA Modules:
  0.0 48.1 jit_solution(18139799246768084528)
XLA Ops:
  0.6 46.4 %shard_map.67 = (bf16[4,96,256]{2,1,0:T(8,128)(2,1)S(1)}, bf16[1,64,4096]{2,1,0:T(8,128)(2,1)S(1)}, bf16[1,64,4096]{2,1,0:T(8,128)(2,1)S(1)}) custom-call(bf16[192,256]{1,0:T(8,128)(2,1)} %q_in.1, bf16[1,64,4096]{2,1,0:T(8,128)(2,1)} %k_in.1, bf16[1,64,4096]{2,1,0:T(8,128)(2,1)} %v_in.1, bf16[1,192,256]{2,1,0:T(8,128)(2,1)} %g_in.1), custom_call_target="tpu_custom_call" | custom-call | flops 2013265920 | bytes 4194304 | tf_op jit(solution)/shard_map/pallas_call | solution.py:446
  47.1 1.1 %shard_map.68 = (f32[192,256]{1,0:T(8,128)}, bf16[1,64,4096]{2,1,0:T(8,128)(2,1)}, bf16[1,64,4096]{2,1,0:T(8,128)(2,1)}) custom-call(bf16[4,96,256]{2,1,0:T(8,128)(2,1)S(1)} %get-tuple-element.6.parts, bf16[1,64,4096]{2,1,0:T(8,128)(2,1)S(1)} %get-tuple-element.7.dk_in, bf16[1,64,4096]{2,1,0:T(8,128)(2,1)S(1)} %get-tuple-element.8.dv_in), custom_call_target="tpu_custom_call" | custom-call | tf_op jit(solution)/shard_map/pallas_call | solution.py:487

commit v7 on v6

--- a/solution.py
+++ b/solution.py
@@ -34,7 +34,7 @@
 def kernel(
     q_in, k_in, v_in, g_in,
     yrecv, dk_out, dv_out,
-    kown, vown, gown, kbuf, vbuf, qbuf, gbuf, pbuf, wbuf, p16, s16, aq, bq, dkst, dvst,
+    kown, vown, gown, kbuf, vbuf, qbuf, gbuf, pbuf, wbuf, sp16, aq, bq, dkst, dvst,
     zsend, zrecv, mstat, tstat, logs, deltas,
     own_sem, ksem, vsem, rsend, rrecv, gsem, lsem, dsem, dksem, dvsem, zsem, zown, ysem,
 ):
@@ -171,7 +171,6 @@
         remote(src.at[:, cols_of(k, 1 - core)], buf.at[pos_of(k, core)], sem.at[0], sem.at[1], where).start()
 
     spread(kown, kbuf, ksem)
-    spread(vown, vbuf, vsem)
     for copy in own[1:]:
         copy.start()
 
@@ -181,6 +180,8 @@
 
 
     for h in range(1, 4):
+        if h == 2:
+            spread(vown, vbuf, vsem)
         for part in range(3):
             for side in range(2):
 
@@ -205,7 +206,7 @@
         p = jnp.exp(s - top)
         total = jnp.sum(p, axis=0, keepdims=True)
         pbuf[i] = p
-        p16[d, :, rows] = p.astype(BF16)
+        sp16[d, :, pl.ds(pl.multiple_of(R + w * WIDE, WIDE), WIDE)] = p.astype(BF16)
         mstat[d, :, rows] = top
         tstat[d, :, rows] = total
         logs[z, d, :, rows] = top + jnp.log(total)
@@ -218,7 +219,7 @@
 
     def settle(d, w):
         i, _, rows, _ = place(d, w)
-        s16[d, :, rows] = (pbuf[i] * (wbuf[i] - deltas[z, d, :, rows])).astype(BF16)
+        sp16[d, :, rows] = (pbuf[i] * (wbuf[i] - deltas[z, d, :, rows])).astype(BF16)
 
     late = lax.div(lax.rem(z, OWNERS), 2)
     early = 1 - late
@@ -263,8 +264,8 @@
     for d in range(CORES):
         docs = pl.ds(d * HERE, HERE)
         settle(d, late)
-        aq[d] = dot(s16[d], kbuf[docs, :], ((0,), (0,)))
-        bq[d] = dot(p16[d], kbuf[docs, :], ((0,), (0,)))
+        aq[d] = dot(sp16[d, :, :R], kbuf[docs, :], ((0,), (0,)))
+        bq[d] = dot(sp16[d, :, R:], kbuf[docs, :], ((0,), (0,)))
 
     def columns(rows):
         return jnp.concatenate(rows + [jnp.zeros((8 - len(rows), R), F32)], axis=0).T
@@ -299,7 +300,7 @@
 
     def value_part(d):
         rows = gbuf[d * R : (d + 1) * R, :].astype(F32) * factor[:, d : d + 1]
-        return dot(p16[d], rows.astype(BF16), ((1,), (0,)))
+        return dot(sp16[d, :, R:], rows.astype(BF16), ((1,), (0,)))
 
     back(dvst, dv_out, dvsem, 0, value_part(0))
 
@@ -315,7 +316,7 @@
     change = columns(changes)
 
     def z_copy(b, c):
-        src = zsend.at[b, pl.ds(c * HALF, HALF)]
+        src = zsend.at[b, pl.ds(pl.multiple_of(c * HALF, 32), HALF)]
         where = (first_core + c, k * Z + core * OWNERS + b)
         return remote(src, zrecv.at[z], zsem.at[0], zsem.at[1], where)
 
@@ -330,8 +331,8 @@
 
         @pl.when(core * OWNERS + b != z)
         def _(b=b):
-            for c in range(CORES):
-                z_copy(b, c).start()
+            for other in range(CORES):
+                z_copy(b, lax.rem(core + 1 + other, CORES)).start()
 
     @pl.when(core == home)
     def _():
@@ -343,7 +344,7 @@
         rows = qbuf[...].astype(F32)
         main = (rows * (factor[:, d : d + 1] * SCALE)).astype(BF16)
         rest = (rows * (change[:, d : d + 1] * SCALE)).astype(BF16)
-        return dot(s16[d], main, ((1,), (0,))) + dot(p16[d], rest, ((1,), (0,)))
+        return dot(sp16[d], jnp.concatenate([main, rest], axis=0), ((1,), (0,)))
 
     back(dvst, dv_out, dvsem, 1, value_part(1))
     for d in range(CORES):
@@ -462,8 +463,7 @@
             pltpu.VMEM((CORES * R, DH), BF16),
             pltpu.VMEM((2 * CORES, HERE, WIDE), F32),
             pltpu.VMEM((2 * CORES, HERE, WIDE), F32),
-            pltpu.VMEM((CORES, HERE, R), BF16),
-            pltpu.VMEM((CORES, HERE, R), BF16),
+            pltpu.VMEM((CORES, HERE, 2 * R), BF16),
             pltpu.VMEM((CORES, R, DH), F32),
             pltpu.VMEM((CORES, R, DH), F32),
             pltpu.VMEM((CORES * HERE, DH), BF16),

time: 48.9 us -> 48.7 us (level)
  no operation moved by 1% of the time
where the time goes in v7:
time: 48.7 us; the launch traced here: 48.1 us
  Pallas kernels  47.5 us (98%)
  between operations  0.64 us (1%)
    pallas_call x1, Pallas kernels, on_device(): pl.pallas_call(kernel, out_shape=(pltpu.VMEM((DOCS, HALF, DH), BF16), plt...  46.4 us
    pallas_call x1, Pallas kernels, on_device(): pl.pallas_call(finish, out_shape=(jax.ShapeDtypeStruct((BLOCK, DH), F32),...  1.05 us

profile of v7, /device:TPU:1, one launch (start us, length us, event | category | flops | bytes accessed | tf_op | source)
XLA Modules:
  0.0 48.1 jit_solution(2167859582438833640)
XLA Ops:
  0.6 46.4 %shard_map.67 = (bf16[4,96,256]{2,1,0:T(8,128)(2,1)S(1)}, bf16[1,64,4096]{2,1,0:T(8,128)(2,1)S(1)}, bf16[1,64,4096]{2,1,0:T(8,128)(2,1)S(1)}) custom-call(bf16[192,256]{1,0:T(8,128)(2,1)} %q_in.1, bf16[1,64,4096]{2,1,0:T(8,128)(2,1)} %k_in.1, bf16[1,64,4096]{2,1,0:T(8,128)(2,1)} %v_in.1, bf16[1,192,256]{2,1,0:T(8,128)(2,1)} %g_in.1), custom_call_target="tpu_custom_call" | custom-call | flops 2013265920 | bytes 4194304 | tf_op jit(solution)/shard_map/pallas_call | solution.py:447
  47.1 1.1 %shard_map.68 = (f32[192,256]{1,0:T(8,128)}, bf16[1,64,4096]{2,1,0:T(8,128)(2,1)}, bf16[1,64,4096]{2,1,0:T(8,128)(2,1)}) custom-call(bf16[4,96,256]{2,1,0:T(8,128)(2,1)S(1)} %get-tuple-element.6.parts, bf16[1,64,4096]{2,1,0:T(8,128)(2,1)S(1)} %get-tuple-element.7.dk_in, bf16[1,64,4096]{2,1,0:T(8,128)(2,1)S(1)} %get-tuple-element.8.dv_in), custom_call_target="tpu_custom_call" | custom-call | tf_op jit(solution)/shard_map/pallas_call | solution.py:487
